TPU v7x, 256 devices: a whole 4x4x8 slice. The times are simulated.
256 devices in a mesh: dp: 16 (over z, core), vocab: 16 (over y, x).
Axes of the slice: x: 4, y: 4, z: 8, core: 2. Of those that a mesh axis runs over, the one named last changes fastest.
Arguments:
- hidden: bfloat16 [256, 7168], P('dp'), may hold values from -400 to 400, as said below
- head_table: bfloat16 [7168, 106496], P('dp', 'vocab'), may hold values from -1 to 1
- embed_table: bfloat16 [106496, 7168], P('vocab', 'dp'), may hold values from -384 to 384
Outputs:
- next_input: bfloat16 [256, 7168], P('dp', 'vocab')
Inputs may be any that keep to these rules, and one draw needn't show every extreme that they name: hidden states of a final norm.
All inputs are finite; a program needn't handle non-finite values.
Results may differ from a plain program's by a relative error of at most 0.02.
Values may be sent and summed in bfloat16 or wider, within the bound.
No kernel may reach another device: no remote copies, remote signals or barrier semaphores. Data moves between devices by JAX's collectives and lax.ppermute only.
A program may use at most 64 MiB of HBM per device.

v0:
```python
import jax
import jax.numpy as jnp
from jax import lax
from jax.sharding import PartitionSpec as P


def row_stats(logits):
    local_top = jnp.max(logits, axis=1, keepdims=True)
    row_top = lax.pmax(local_top, "vocab")
    scaled = jnp.exp(logits - row_top)
    row_total = lax.psum(jnp.sum(scaled, axis=1, keepdims=True), "vocab")
    return (scaled.astype(jnp.bfloat16), row_total)


def on_device(hidden, head_table, embed_table):
    rows_dev = hidden.shape[0]
    slices = lax.all_to_all(hidden, "dp", split_axis=1, concat_axis=0, tiled=True)
    logits = lax.psum(jnp.dot(slices, head_table, preferred_element_type=jnp.float32), "dp")
    weights, all_totals = row_stats(logits)
    partial_value = jnp.dot(weights, embed_table, preferred_element_type=jnp.float32)
    row_total = lax.dynamic_slice_in_dim(all_totals, lax.axis_index("dp") * rows_dev, rows_dev, 0)
    owned_rows = lax.all_to_all(
        partial_value.astype(jnp.bfloat16), "dp", split_axis=0, concat_axis=1, tiled=True
    ).astype(partial_value.dtype)
    summed = lax.psum_scatter(
        owned_rows.astype(jnp.bfloat16), "vocab", scatter_dimension=1, tiled=True
    ).astype(jnp.float32)
    return (summed / row_total).astype(jnp.bfloat16)


def solution(mesh):
    in_specs = (P("dp", None), P("dp", "vocab"), P("vocab", "dp"))
    out_specs = P("dp", "vocab")
    return jax.shard_map(
        on_device, mesh=mesh, in_specs=in_specs, out_specs=out_specs, check_vma=False
    )
```

profile of v0, /device:TPU:16, one launch (start us, length us, event | category | flops | bytes accessed | tf_op | source)
XLA Modules:
  0.0 312.0 jit_solution(18075189115363818814)
XLA Ops:
  6.5 0.0 all-reduce.2.cloned.1.call-start
  6.5 1.3 all_to_all.28
  7.8 0.2 copy.10
  8.0 19.5 %all_to_all.38 = bf16[16,16,448]{2,0,1:T(8,128)(2,1)S(1)} all-to-all(bf16[16,16,448]{2,0,1:T(8,128)(2,1)S(1)} %copy.10), channel_id=1, replica_groups=mesh['dp'=16,'vocab'=16] {'dp'}, dimensions={1} | all-to-all | bytes 458752 | tf_op jit(solution)/shard_map/all_to_all | solution.py:17
  27.5 7.5 %fusion.8 = f32[256,6656]{1,0:T(8,128)} fusion(bf16[256,448]{1,0:T(8,128)(2,1)S(1)} %bitcast.16, bf16[448,6656]{1,0:T(8,128)(2,1)} %param.4), kind=kOutput, calls=%fused_computation.8 | convolution fusion | flops 1526726656 | bytes 13008896 | tf_op jit(solution)/shard_map/dot_general | solution.py:18
  35.0 0.0 all-reduce.2.cloned.1.call-update
  35.0 127.8 %all-reduce.2.cloned.1.call-done = f32[256,6656]{1,0:T(8,128)} async-done(((f32[256,6656]{1,0:T(8,128)}), f32[256,6656]{1,0:T(8,128)}) %all-reduce.2.cloned.1.call-update) | async-done | bytes 6815760 | tf_op jit(solution)/shard_map/psum | solution.py:18
  162.8 3.3 %reduce_max.9 = f32[256]{0:T(256)S(1)} reduce(f32[256,6656]{1,0:T(8,128)} %all-reduce.2.cloned.1.call-done, f32[]{:T(128)} %constant.2.clone.1), dimensions={1}, to_apply=%region_1.0 | reduce | flops 1703680 | bytes 6816772 | tf_op jit(solution)/shard_map/reduce_max | solution.py:8
  166.1 33.3 %pmax.7 = f32[256]{0:T(256)S(1)} all-reduce(f32[256]{0:T(256)S(1)} %reduce_max.9), channel_id=1, replica_groups=mesh['dp'=16,'vocab'=16] {'vocab'}, use_global_device_ids=true, to_apply=%region_2.0 | all-reduce | flops 256 | bytes 2048 | tf_op jit(solution)/shard_map/pmax | solution.py:9
  199.4 6.4 %fusion.5 = bf16[256,448]{0,1:T(8,128)(2,1)S(1)} fusion(bf16[6656,448]{0,1:T(8,128)(2,1)} %param.5, f32[256,6656]{1,0:T(8,128)} %all-reduce.2.cloned.1.call-done, f32[256]{0:T(256)S(1)} %pmax.7), kind=kOutput, calls=%fused_computation.5 | convolution fusion | flops 1530249216 | bytes 13009920 | tf_op jit(solution)/shard_map/dot_general | solution.py:20
  205.9 0.9 copy.11
  206.7 5.4 %all-to-all-start.1 = ((bf16[16,16,448]{2,1,0:T(8,128)(2,1)}), bf16[16,16,448]{2,1,0:T(8,128)(2,1)S(1)}, u32[]{:S(2)}, u32[]{:S(2)}) async-start(bf16[16,16,448]{2,1,0:T(8,128)(2,1)} %bitcast.2), calls=%async_computation.1 | async-start | bytes 524288 | tf_op jit(solution)/shard_map/all_to_all | solution.py:22
  212.2 0.0 reduce-scatter.4.cloned.1.call-start
  212.2 11.1 %all-to-all-done.1 = bf16[16,16,448]{2,1,0:T(8,128)(2,1)S(1)} async-done(((bf16[16,16,448]{2,1,0:T(8,128)(2,1)}), bf16[16,16,448]{2,1,0:T(8,128)(2,1)S(1)}, u32[]{:S(2)}, u32[]{:S(2)}) %all-to-all-start.1) | async-done | bytes 229408 | tf_op jit(solution)/shard_map/all_to_all | solution.py:22
  223.3 1.7 copy.15
  225.0 0.0 reduce-scatter.4.cloned.1.call-update
  225.0 4.0 %fusion = f32[256]{0:T(256)S(1)} fusion(f32[256,6656]{1,0:T(8,128)} %all-reduce.2.cloned.1.call-done, f32[256]{0:T(256)S(1)} %pmax.7), kind=kLoop, calls=%fused_computation.1 | loop fusion | flops 3407616 | bytes 6817792 | tf_op jit(solution)/shard_map/reduce_sum | solution.py:11
  229.0 30.8 %psum.15 = f32[256,1]{0,1:T(1,128)S(1)} all-reduce(f32[256,1]{0,1:T(1,128)S(1)} %bitcast.19), channel_id=1, replica_groups=mesh['dp'=16,'vocab'=16] {'vocab'}, use_global_device_ids=true, to_apply=%region_5.0 | all-reduce | flops 256 | bytes 2048 | tf_op jit(solution)/shard_map/psum | solution.py:11
  259.8 0.1 dynamic-slice_bitcast_fusion
  259.9 43.7 %reduce-scatter.4.cloned.1.call-done = bf16[448,16]{1,0:T(8,128)(2,1)} async-done(((bf16[7168,16]{1,0:T(8,128)(2,1)}), bf16[448,16]{1,0:T(8,128)(2,1)}) %reduce-scatter.4.cloned.1.call-update) | async-done | bytes 14352
  303.5 1.0 copy.14
  304.5 0.7 divide_convert_fusion
Async XLA Ops:
  6.5 156.3 %all-reduce.2.cloned.1.call-start = ((), (), s32[]{:S(2)}) async-start(), calls=%async_computation.3 | async-start | bytes 13631488 | tf_op jit(solution)/shard_map/psum | solution.py:18
  206.7 16.6 %all-to-all-start.1 = ((bf16[16,16,448]{2,1,0:T(8,128)(2,1)}), bf16[16,16,448]{2,1,0:T(8,128)(2,1)S(1)}, u32[]{:S(2)}, u32[]{:S(2)}) async-start(bf16[16,16,448]{2,1,0:T(8,128)(2,1)} %bitcast.2), calls=%async_computation.1 | async-start | bytes 524288 | tf_op jit(solution)/shard_map/all_to_all | solution.py:22
  212.2 91.4 %reduce-scatter.4.cloned.1.call-start = ((), (), s32[]{:S(2)}) async-start(), calls=%async_computation.4 | async-start | bytes 1949696
Sparse Core Ops, SparseCore 0:
  35.2 127.5 all-reduce.1
  225.2 78.3 reduce-scatter.3
where the time goes:
time: 313 us; the launch traced here: 312 us
  waiting for transfers between devices  183 us (58%)
  blocking collectives  83.6 us (27%)
  matrix products  13.9 us (4%)
  between operations  13.4 us (4%)
  other arithmetic  8.03 us (3%)
  starting transfers between devices  5.47 us (2%)
  local copies, waits for them, and re-layouts  5 us (2%)
    psum x1, waiting for transfers between devices, on_device(): lax.psum(jnp.dot(slices, head_table, preferred_element_type=jnp.float32),...  128 us
    unnamed x3, waiting for transfers between devices  43.7 us
    pmax x1, blocking collectives, row_stats(): row_top = lax.pmax(local_top, 'vocab')  33.3 us
    psum x1, blocking collectives, row_stats(): row_total = lax.psum(jnp.sum(scaled, axis=1, keepdims=True), 'vocab')  30.8 us
    all_to_all x1, blocking collectives, on_device(): lax.all_to_all(hidden, 'dp', split_axis=1, concat_axis=0, tiled=True)  19.5 us
    all_to_all x1, waiting for transfers between devices, on_device(): lax.all_to_all(partial_value.astype(jnp.bfloat16), 'dp', split_axis=0, co...  11.1 us
    dot_general x1, matrix products, on_device(): jnp.dot(slices, head_table, preferred_element_type=jnp.float32)  7.5 us
    dot_general x1, matrix products, on_device(): jnp.dot(weights, embed_table, preferred_element_type=jnp.float32)  6.45 us
  transfers between devices with their start and end apart: 3, of which 3 were waited for; matrix products, arithmetic and copies ran while one was open for 1% of the time, Pallas kernels for 0%

commit v1 on v0

v1 whole, which is shorter than its diff:
```python
import jax
import jax.numpy as jnp
from jax import lax
from jax.sharding import PartitionSpec as P

WIRE = jnp.float16
SCALE = 1.0 / 64.0
BF16, F32 = jnp.bfloat16, jnp.float32


def pieces(value, width):
    parts = []
    for _ in range(3):
        head = lax.reduce_precision(value, 8, 7)
        parts.append(head.astype(BF16))
        value = value - head
    return parts


def stat_block(top, total, width):
    block = jnp.concatenate(pieces(top, width) + pieces(total, width), -1)
    pad = [(0, 0)] * (block.ndim - 1) + [(0, width - 6)]
    return jnp.pad(block, pad)


def read_stats(block):
    block = block.astype(F32)
    top = block[..., 0:1] + block[..., 1:2] + block[..., 2:3]
    total = block[..., 3:4] + block[..., 4:5] + block[..., 5:6]
    return top, total


def on_device(hidden, head_table, embed_table):
    me = lax.axis_index("dp")
    z, core = me // 2, me % 2
    size = lax.axis_size("dp")
    chips = size // 2
    rows_dev = hidden.shape[0]
    feats, vocab = head_table.shape
    half = vocab // 2
    cut = (half // 256) * 128

    swap_pairs = [(i, i ^ 1) for i in range(size)]
    up_pairs = [(i, (i + 2) % size) for i in range(size)]
    down_pairs = [(i, (i - 2) % size) for i in range(size)]
    swap = lambda x: lax.ppermute(x, "dp", swap_pairs)
    up = lambda x: lax.ppermute(x, "dp", up_pairs)
    down = lambda x: lax.ppermute(x, "dp", down_pairs)
    dot = lambda a, b: jnp.dot(a, b, preferred_element_type=F32)
    enc = lambda x: (x * SCALE).astype(WIRE)
    dec = lambda x: x.astype(F32) * (1.0 / SCALE)

    mine, other = core * half, (1 - core) * half
    slices = lax.all_to_all(hidden, "dp", split_axis=1, concat_axis=0, tiled=True)
    head_other = swap(lax.dynamic_slice_in_dim(head_table, other, half, 1))
    slices_other = swap(slices)
    embed_other = swap(lax.dynamic_slice_in_dim(embed_table, other, half, 0))
    head_mine = lax.dynamic_slice_in_dim(head_table, mine, half, 1)
    embed_mine = lax.dynamic_slice_in_dim(embed_table, mine, half, 0)

    def batch_rows(x, b):
        return x.reshape(chips, 2, rows_dev, feats)[:, b].reshape(chips * rows_dev, feats)

    def ring_sum(logits):
        part = lambda o: lax.dynamic_index_in_dim(logits, (z + o) % chips, 0, keepdims=False)
        far = part(4)
        a = up(enc(far[:, :cut]))
        b = down(enc(far[:, cut:]))
        p3, m3 = part(3), part(-3)
        a = up(enc(jnp.concatenate([p3[:, :cut] + dec(a), p3[:, cut:]], 1)))
        b = down(enc(jnp.concatenate([m3[:, :cut], m3[:, cut:] + dec(b)], 1)))
        a = up(enc(part(2) + dec(a)))
        b = down(enc(part(-2) + dec(b)))
        a = up(enc(part(1) + dec(a)))
        b = down(enc(part(-1) + dec(b)))
        return part(0) + dec(a) + dec(b)

    def ring_gather(block):
        buf = jnp.zeros((chips,) + block.shape, block.dtype)
        put = lambda buf, x, o, c: lax.dynamic_update_slice(buf, x[None], ((z + o) % chips, 0, c))
        buf = put(buf, block, 0, 0)
        a, b = block, block
        for step in range(1, 4):
            a, b = up(a), down(b)
            buf = put(put(buf, a, -step, 0), b, step, 0)
        a, b = up(a[:, :cut]), down(b[:, cut:])
        buf = put(put(buf, a, -4, 0), b, 4, cut)
        return buf.reshape(chips * block.shape[0], block.shape[1])

    outs = []
    for b in range(2):
        logits = dot(batch_rows(slices, b), head_mine) + dot(batch_rows(slices_other, b), head_other)
        full = ring_sum(logits.reshape(chips, rows_dev, half))
        top = jnp.max(full, axis=1, keepdims=True)
        scaled = jnp.exp(full - top)
        total = jnp.sum(scaled, axis=1, keepdims=True)
        block = jnp.concatenate([scaled.astype(BF16), stat_block(top, total, 128)], 1)
        block = ring_gather(block)
        weights, stats = block[:, :half], block[:, half : half + 64]
        value_other = dot(weights, embed_other).astype(BF16)
        from_other = swap(jnp.concatenate([value_other, stats], 1))
        value_mine = dot(weights, embed_mine)
        top_m, tot_m = read_stats(stats)
        top_o, tot_o = read_stats(from_other[:, feats:])
        top = jnp.maximum(top_m, top_o)
        f_m, f_o = jnp.exp(top_m - top), jnp.exp(top_o - top)
        value = value_mine * f_m + from_other[:, :feats].astype(F32) * f_o
        out = jnp.concatenate([value.astype(BF16), stat_block(top, tot_m * f_m + tot_o * f_o, 64)], 1)
        outs.append(out.reshape(chips, rows_dev, feats + 64))

    blocks = jnp.stack(outs, 1).reshape(size, rows_dev, feats + 64)
    got = lax.all_to_all(blocks, "vocab", 0, 0)
    tops, tots = read_stats(got[:, :, feats:])
    factor = jnp.exp(tops - jnp.max(tops, axis=0, keepdims=True))
    row_total = jnp.sum(tots * factor, axis=0)
    mixture = jnp.sum(got[:, :, :feats].astype(F32) * factor, axis=0)
    result = (mixture / row_total).astype(BF16)
    flip = [(d * size + v, v * size + d) for d in range(size) for v in range(size)]
    return lax.ppermute(result, ("dp", "vocab"), flip)


def solution(mesh):
    in_specs = (P("dp", None), P("dp", "vocab"), P("vocab", "dp"))
    out_specs = P("dp", "vocab")
    return jax.shard_map(
        on_device, mesh=mesh, in_specs=in_specs, out_specs=out_specs, check_vma=False
    )
```

time: 313 us -> 145 us (0.46)
  waiting for transfers between devices: 183 us -> 30 us
  blocking collectives: 83.6 us -> 13.4 us
  starting transfers between devices: 5.47 us -> 61.8 us
  between operations: 13.4 us -> 0.8 us
  local copies, waits for them, and re-layouts: 5 us -> 17.1 us
  other arithmetic: 8.03 us -> 4.84 us
    psum x1 -> x0, waiting for transfers between devices: 128 us -> none  [on_device(): lax.psum(jnp.dot(slices, head_table, preferred_element_type=jnp.float32),...]
    ppermute x0 -> x38, starting transfers between devices: none -> 53.2 us  [the longest x16 36.8 us: on_device(): down = lambda x: lax.ppermute(x, 'dp', down_pairs)]
    unnamed x3 -> x0, waiting for transfers between devices: 43.7 us -> none
    pmax x1 -> x0, blocking collectives: 33.3 us -> none  [row_stats(): row_top = lax.pmax(local_top, 'vocab')]
    psum x1 -> x0, blocking collectives: 30.8 us -> none  [row_stats(): row_total = lax.psum(jnp.sum(scaled, axis=1, keepdims=True), 'vocab')]
    ppermute x0 -> x38, waiting for transfers between devices: none -> 19 us  [the longest x16 10.6 us: on_device(): up = lambda x: lax.ppermute(x, 'dp', up_pairs)]
    dynamic_update_slice x0 -> x16, local copies, waits for them, and re-layouts: none -> 6.25 us  [ring_gather(): lax.dynamic_update_slice(buf, x[None], ((z + o) % chips, 0, c))]
    all_to_all x1, blocking collectives: 19.5 us -> 13.4 us  [on_device(): got = lax.all_to_all(blocks, 'vocab', 0, 0)]
  transfers between devices with their start and end apart: 3 -> 39, of which waited for: 3 -> 10; matrix products, arithmetic and copies ran while one was open for 1% -> 19% of each run, Pallas kernels for 0% -> 0%
where the time goes in v1:
time: 145 us; the launch traced here: 144 us
  starting transfers between devices  61.8 us (43%)
  waiting for transfers between devices  30 us (21%)
  local copies, waits for them, and re-layouts  17.1 us (12%)
  matrix products  16.4 us (11%)
  blocking collectives  13.4 us (9%)
  other arithmetic  4.84 us (3%)
    ppermute x16, starting transfers between devices, on_device(): down = lambda x: lax.ppermute(x, 'dp', down_pairs)  36.8 us
    dot_general x8, matrix products, on_device(): dot = lambda a, b: jnp.dot(a, b, preferred_element_type=F32)  16.4 us
    all_to_all x1, blocking collectives, on_device(): got = lax.all_to_all(blocks, 'vocab', 0, 0)  13.4 us
    all_to_all x1, waiting for transfers between devices, on_device(): lax.all_to_all(hidden, 'dp', split_axis=1, concat_axis=0, tiled=True)  11 us
    ppermute x16, waiting for transfers between devices, on_device(): up = lambda x: lax.ppermute(x, 'dp', up_pairs)  10.6 us
    all_to_all x1, starting transfers between devices, on_device(): lax.all_to_all(hidden, 'dp', split_axis=1, concat_axis=0, tiled=True)  8.68 us
    ppermute x1, starting transfers between devices, on_device(): return lax.ppermute(result, ('dp', 'vocab'), flip)  7.81 us
    ppermute x16, starting transfers between devices, on_device(): up = lambda x: lax.ppermute(x, 'dp', up_pairs)  6.95 us
  transfers between devices with their start and end apart: 39, of which 10 were waited for; matrix products, arithmetic and copies ran while one was open for 19% of the time, Pallas kernels for 0%

profile of v1, /device:TPU:16, one launch (start us, length us, event | category | flops | bytes accessed | tf_op | source)
XLA Modules:
  0.0 144.4 jit_solution(7894632289622076439)
XLA Ops:
  0.0 3.7 %constant_dynamic-slice_fusion.1 = bf16[448,3328]{1,0:T(8,128)(2,1)} fusion(bf16[448,6656]{1,0:T(8,128)(2,1)} %param.4, s32[]{:T(128)S(6)} %select_n.160), kind=kLoop, calls=%fused_computation.130 | loop fusion | bytes 5963780 | tf_op jit(solution)/shard_map/dynamic_slice | solution.py:55
  4.0 0.9 copy.85
  4.8 8.7 %all-to-all-start = ((bf16[16,16,448]{2,0,1:T(8,128)(2,1)}), bf16[16,16,448]{2,0,1:T(8,128)(2,1)S(1)}, u32[]{:S(2)}, u32[]{:S(2)}) async-start(bf16[16,16,448]{2,0,1:T(8,128)(2,1)} %copy.85), calls=%async_computation | async-start | bytes 524288 | tf_op jit(solution)/shard_map/all_to_all | solution.py:54
  13.7 11.0 %all-to-all-done = bf16[16,16,448]{2,0,1:T(8,128)(2,1)S(1)} async-done(((bf16[16,16,448]{2,0,1:T(8,128)(2,1)}), bf16[16,16,448]{2,0,1:T(8,128)(2,1)S(1)}, u32[]{:S(2)}, u32[]{:S(2)}) %all-to-all-start) | async-done | bytes 229408 | tf_op jit(solution)/shard_map/all_to_all | solution.py:54
  24.7 0.9 collective-permute-start.1
  25.7 2.5 %fusion.6 = f32[3328,128]{0,1:T(8,128)S(1)} fusion(bf16[128,448]{1,0:T(8,128)(2,1)S(1)} %bitcast.192, bf16[448,6656]{1,0:T(8,128)(2,1)} %param.4, s32[]{:T(128)S(6)} %select_n.159), kind=kOutput, calls=%fused_computation.8 | convolution fusion | flops 381681664 | bytes 4800516 | tf_op jit(solution)/shard_map/dot_general | solution.py:49
  28.1 2.5 %fusion.4 = f32[3328,128]{0,1:T(8,128)S(1)} fusion(bf16[128,448]{1,0:T(8,128)(2,1)S(1)} %bitcast.191, bf16[448,6656]{1,0:T(8,128)(2,1)} %param.4, s32[]{:T(128)S(6)} %select_n.159), kind=kOutput, calls=%fused_computation.6 | convolution fusion | flops 381681664 | bytes 4800516 | tf_op jit(solution)/shard_map/dot_general | solution.py:49
  31.5 2.0 %collective-permute-start.20 = (f16[16,1664]{1,0:T(8,128)(2,1)S(1)}, f16[16,1664]{1,0:T(8,128)(2,1)S(1)}, u32[]{:S(2)}, u32[]{:S(2)}) collective-permute-start(f16[16,1664]{1,0:T(8,128)(2,1)S(1)} %get-tuple-element.49), channel_id=1, source_target_pairs={{0,32},{16,48},{32,64},{48,80},{64,96},{80,112},{96,128},{112,144}... | collective-permute-start | bytes 159752 | tf_op jit(solution)/shard_map/ppermute | solution.py:47
  34.3 1.4 collective-permute-start.6
  35.7 0.7 collective-permute-start.2
  36.5 2.6 %collective-permute-start.25 = (f16[16,3328]{1,0:T(8,128)(2,1)S(1)}, f16[16,3328]{1,0:T(8,128)(2,1)S(1)}, u32[]{:S(2)}, u32[]{:S(2)}) collective-permute-start(f16[16,3328]{1,0:T(8,128)(2,1)S(1)} %fusion.37), channel_id=1, source_target_pairs={{0,224},{16,240},{32,0},{48,16},{64,32},{80,48},{96,64},{112,80},{... | collective-permute-start | bytes 319496 | tf_op jit(solution)/shard_map/ppermute | solution.py:48
  39.3 3.3 %collective-permute-start.7 = (f16[16,3328]{1,0:T(8,128)(2,1)S(1)}, f16[16,3328]{1,0:T(8,128)(2,1)S(1)}, u32[]{:S(2)}, u32[]{:S(2)}) collective-permute-start(f16[16,3328]{1,0:T(8,128)(2,1)S(1)} %fusion.35), channel_id=1, source_target_pairs={{0,224},{16,240},{32,0},{48,16},{64,32},{80,48},{96,64},{112,80},{... | collective-permute-start | bytes 319496 | tf_op jit(solution)/shard_map/ppermute | solution.py:48
  42.7 2.7 %collective-permute-done.21 = f16[16,3328]{1,0:T(8,128)(2,1)S(1)} collective-permute-done((f16[16,3328]{1,0:T(8,128)(2,1)S(1)}, f16[16,3328]{1,0:T(8,128)(2,1)S(1)}, u32[]{:S(2)}, u32[]{:S(2)}) %collective-permute-start.21) | collective-permute-done | bytes 106528 | tf_op jit(solution)/shard_map/ppermute | solution.py:47
  45.5 3.5 %collective-permute-done.3 = f16[16,3328]{1,0:T(8,128)(2,1)S(1)} collective-permute-done((f16[16,3328]{1,0:T(8,128)(2,1)S(1)}, f16[16,3328]{1,0:T(8,128)(2,1)S(1)}, u32[]{:S(2)}, u32[]{:S(2)}) %collective-permute-start.3) | collective-permute-done | bytes 106528 | tf_op jit(solution)/shard_map/ppermute | solution.py:47
  49.4 3.1 %collective-permute-done.22 = f16[16,3328]{1,0:T(8,128)(2,1)S(1)} collective-permute-done((f16[16,3328]{1,0:T(8,128)(2,1)S(1)}, f16[16,3328]{1,0:T(8,128)(2,1)S(1)}, u32[]{:S(2)}, u32[]{:S(2)}) %collective-permute-start.22) | collective-permute-done | bytes 106528 | tf_op jit(solution)/shard_map/ppermute | solution.py:47
  52.8 1.9 %collective-permute-start.23 = (f16[16,3328]{1,0:T(8,128)(2,1)S(1)}, f16[16,3328]{1,0:T(8,128)(2,1)S(1)}, u32[]{:S(2)}, u32[]{:S(2)}) collective-permute-start(f16[16,3328]{1,0:T(8,128)(2,1)S(1)} %get-tuple-element.28), channel_id=1, source_target_pairs={{0,32},{16,48},{32,64},{48,80},{64,96},{80,112},{96,128},{112,144}... | collective-permute-start | bytes 319496 | tf_op jit(solution)/shard_map/ppermute | solution.py:47
  55.4 0.8 collective-permute-start.8
  56.2 1.3 collective-permute-start.5
  57.5 0.7 collective-permute-done.26
  58.3 1.3 collective-permute-start.27
  59.5 1.5 %collective-permute-done.8 = f16[16,3328]{1,0:T(8,128)(2,1)S(1)} collective-permute-done((f16[16,3328]{1,0:T(8,128)(2,1)S(1)}, f16[16,3328]{1,0:T(8,128)(2,1)S(1)}, u32[]{:S(2)}, u32[]{:S(2)}) %collective-permute-start.8) | collective-permute-done | bytes 106528 | tf_op jit(solution)/shard_map/ppermute | solution.py:48
  61.1 1.2 collective-permute-start.9
  62.2 1.8 %constant_dynamic-slice_fusion = bf16[3328,448]{0,1:T(8,128)(2,1)} fusion(bf16[6656,448]{0,1:T(8,128)(2,1)S(1)} %bitcast.185, s32[]{:T(128)S(6)} %select_n.160), kind=kLoop, calls=%fused_computation.128 | loop fusion | bytes 5963780 | tf_op jit(solution)/shard_map/dynamic_slice | solution.py:57
  64.0 1.9 %collective-permute-done.9 = f16[16,3328]{1,0:T(8,128)(2,1)} collective-permute-done((f16[16,3328]{1,0:T(8,128)(2,1)S(1)}, f16[16,3328]{1,0:T(8,128)(2,1)}, u32[]{:S(2)}, u32[]{:S(2)}) %collective-permute-start.9) | collective-permute-done | bytes 106528 | tf_op jit(solution)/shard_map/ppermute | solution.py:48
  65.9 1.4 fusion.103
  68.5 3.2 %collective-permute-start.11 = (bf16[16,3456]{1,0:T(8,128)(2,1)}, bf16[16,3456]{1,0:T(8,128)(2,1)S(1)}, u32[]{:S(2)}, u32[]{:S(2)}) collective-permute-start(bf16[16,3456]{1,0:T(8,128)(2,1)} %fusion.65), channel_id=1, source_target_pairs={{0,224},{16,240},{32,0},{48,16},{64,32},{80,48},{96,64},{112,80},{... | collective-permute-start | bytes 331784 | tf_op jit(solution)/shard_map/ppermute | solution.py:48
  72.1 3.2 %collective-permute-start.29 = (bf16[16,3456]{1,0:T(8,128)(2,1)S(1)}, bf16[16,3456]{1,0:T(8,128)(2,1)S(1)}, u32[]{:S(2)}, u32[]{:S(2)}) collective-permute-start(bf16[16,3456]{1,0:T(8,128)(2,1)S(1)} %fusion.66), channel_id=1, source_target_pairs={{0,224},{16,240},{32,0},{48,16},{64,32},{80,48},{96,64},{112,80},{... | collective-permute-start | bytes 331784 | tf_op jit(solution)/shard_map/ppermute | solution.py:48
  75.4 1.0 broadcast.39.clone
  77.1 0.9 bitcast_dynamic-update-slice_fusion.12
  78.0 3.3 %collective-permute-start.13 = (bf16[16,3456]{1,0:T(8,128)(2,1)S(1)}, bf16[16,3456]{1,0:T(8,128)(2,1)S(1)}, u32[]{:S(2)}, u32[]{:S(2)}) collective-permute-start(bf16[16,3456]{1,0:T(8,128)(2,1)S(1)} %collective-permute-done.11), channel_id=1, source_target_pairs={{0,224},{16,240},{32,0},{48,16},{64,32},{80,48},{96,64},{112,80},{... | collective-permute-start | bytes 331784 | tf_op jit(solution)/shard_map/ppermute | solution.py:48
  81.4 0.7 bitcast_dynamic-update-slice_fusion.5
  82.1 3.2 %collective-permute-start.31 = (bf16[16,3456]{1,0:T(8,128)(2,1)S(1)}, bf16[16,3456]{1,0:T(8,128)(2,1)S(1)}, u32[]{:S(2)}, u32[]{:S(2)}) collective-permute-start(bf16[16,3456]{1,0:T(8,128)(2,1)S(1)} %collective-permute-done.29), channel_id=1, source_target_pairs={{0,224},{16,240},{32,0},{48,16},{64,32},{80,48},{96,64},{112,80},{... | collective-permute-start | bytes 331784 | tf_op jit(solution)/shard_map/ppermute | solution.py:48
  86.0 3.3 %collective-permute-start.15 = (bf16[16,3456]{1,0:T(8,128)(2,1)S(1)}, bf16[16,3456]{1,0:T(8,128)(2,1)S(1)}, u32[]{:S(2)}, u32[]{:S(2)}) collective-permute-start(bf16[16,3456]{1,0:T(8,128)(2,1)S(1)} %collective-permute-done.13), channel_id=1, source_target_pairs={{0,224},{16,240},{32,0},{48,16},{64,32},{80,48},{96,64},{112,80},{... | collective-permute-start | bytes 331784 | tf_op jit(solution)/shard_map/ppermute | solution.py:48
  89.4 0.7 bitcast_dynamic-update-slice_fusion.3
  90.1 3.2 %collective-permute-start.33 = (bf16[16,3456]{1,0:T(8,128)(2,1)S(1)}, bf16[16,3456]{1,0:T(8,128)(2,1)S(1)}, u32[]{:S(2)}, u32[]{:S(2)}) collective-permute-start(bf16[16,3456]{1,0:T(8,128)(2,1)S(1)} %collective-permute-done.31), channel_id=1, source_target_pairs={{0,224},{16,240},{32,0},{48,16},{64,32},{80,48},{96,64},{112,80},{... | collective-permute-start | bytes 331784 | tf_op jit(solution)/shard_map/ppermute | solution.py:48
  93.3 0.7 bitcast_dynamic-update-slice_fusion.2
  94.1 3.3 %collective-permute-start.17 = (bf16[16,1792]{1,0:T(8,128)(2,1)S(1)}, bf16[16,1792]{1,0:T(8,128)(2,1)S(1)}, u32[]{:S(2)}, u32[]{:S(2)}) collective-permute-start(bf16[16,1792]{1,0:T(8,128)(2,1)S(1)} %slice.249), channel_id=1, source_target_pairs={{0,224},{16,240},{32,0},{48,16},{64,32},{80,48},{96,64},{112,80},{... | collective-permute-start | bytes 172040 | tf_op jit(solution)/shard_map/ppermute | solution.py:48
  97.5 3.3 %collective-permute-start.35 = (bf16[16,1792]{1,0:T(8,128)(2,1)S(1)}, bf16[16,1792]{1,0:T(8,128)(2,1)S(1)}, u32[]{:S(2)}, u32[]{:S(2)}) collective-permute-start(bf16[16,1792]{1,0:T(8,128)(2,1)S(1)} %slice.275), channel_id=1, source_target_pairs={{0,224},{16,240},{32,0},{48,16},{64,32},{80,48},{96,64},{112,80},{... | collective-permute-start | bytes 172040 | tf_op jit(solution)/shard_map/ppermute | solution.py:48
  101.5 0.7 bitcast_dynamic-update-slice_fusion
  103.5 0.9 copy-done.2
  104.5 2.1 %convolution_convert_fusion.1 = bf16[128,448]{0,1:T(8,128)(2,1)S(1)} fusion(bf16[3328,448]{0,1:T(8,128)(2,1)S(1)} %collective-permute-done.18, bf16[128,3456]{1,0:T(8,128)(2,1)} %bitcast.182), kind=kOutput, calls=%fused_computation.17 | convolution fusion | flops 381739008 | bytes 3948544 | tf_op jit(solution)/shard_map/dot_general | solution.py:49
  107.3 2.1 %convolution_convert_fusion = bf16[128,448]{0,1:T(8,128)(2,1)S(1)} fusion(bf16[3328,448]{0,1:T(8,128)(2,1)S(1)} %collective-permute-done.18, bf16[128,3456]{1,0:T(8,128)(2,1)} %bitcast.57), kind=kOutput, calls=%fused_computation.16 | convolution fusion | flops 381739008 | bytes 3948544 | tf_op jit(solution)/shard_map/dot_general | solution.py:49
  109.4 0.8 slice.277
  110.9 3.0 %fusion.20 = bf16[128,448]{0,1:T(8,128)(2,1)S(1)} fusion(bf16[6656,448]{0,1:T(8,128)(2,1)} %param.5, s32[]{:T(128)S(6)} %select_n.159, bf16[128,3456]{1,0:T(8,128)(2,1)} %bitcast.183, bf16[128,512]{0,1:T(8,128)(2,1)S(1)} %collective-permute-done.19, f32[128]{0:T(128)S(1)} %get-tuple-element.53, f32[128]{0:T(128)S(1)} %get-tuple-element.9), kind=kOutput, calls=%fused_computation.14 | convolution fusion | flops 381968384 | bytes 4064260 | tf_op jit(solution)/shard_map/dot_general | solution.py:49
  114.3 3.0 %fusion.23 = bf16[128,448]{0,1:T(8,128)(2,1)S(1)} fusion(bf16[6656,448]{0,1:T(8,128)(2,1)} %param.5, s32[]{:T(128)S(6)} %select_n.159, bf16[128,3456]{1,0:T(8,128)(2,1)} %bitcast.57, bf16[128,512]{0,1:T(8,128)(2,1)S(1)} %collective-permute-done.36, f32[128]{0:T(128)S(1)} %get-tuple-element.59, f32[128]{0:T(128)S(1)} %get-tuple-element.16), kind=kOutput, calls=%fused_computation.15 | convolution fusion | flops 381968384 | bytes 4064260 | tf_op jit(solution)/shard_map/dot_general | solution.py:49
  117.5 13.4 %all_to_all.24 = bf16[16,16,512]{2,1,0:T(8,128)(2,1)S(1)} all-to-all(bf16[16,16,512]{2,1,0:T(8,128)(2,1)S(1)} %bitcast.188), channel_id=1, replica_groups=mesh['dp'=16,'vocab'=16] {'vocab'}, dimensions={0} | all-to-all | bytes 524288 | tf_op jit(solution)/shard_map/all_to_all | solution.py:112
  131.7 7.8 %collective-permute-start.37 = (bf16[16,448]{1,0:T(8,128)(2,1)S(1)}, bf16[16,448]{1,0:T(8,128)(2,1)S(1)}, u32[]{:S(2)}, u32[]{:S(2)}) collective-permute-start(bf16[16,448]{1,0:T(8,128)(2,1)S(1)} %divide_convert_fusion), channel_id=1, source_target_pairs={{0,0},{1,16},{2,32},{3,48},{4,64},{5,80},{6,96},{7,112},{8,128},{9... | collective-permute-start | bytes 43016 | tf_op jit(solution)/shard_map/ppermute | solution.py:119
  139.6 4.2 %collective-permute-done.37 = bf16[16,448]{1,0:T(8,128)(2,1)S(1)} collective-permute-done((bf16[16,448]{1,0:T(8,128)(2,1)S(1)}, bf16[16,448]{1,0:T(8,128)(2,1)S(1)}, u32[]{:S(2)}, u32[]{:S(2)}) %collective-permute-start.37) | collective-permute-done | bytes 14368 | tf_op jit(solution)/shard_map/ppermute | solution.py:119
  (143 shorter events, 12.7 us)
Async XLA Ops:
  0.0 3.7 %copy-start.3 = (bf16[16,7168]{1,0:T(8,128)(2,1)S(1)}, bf16[16,7168]{1,0:T(8,128)(2,1)}, u32[]{:S(2)}) copy-start(bf16[16,7168]{1,0:T(8,128)(2,1)} %param.3) | copy-start | bytes 688132
  3.7 27.0 %collective-permute-start = (bf16[448,3328]{1,0:T(8,128)(2,1)}, bf16[448,3328]{1,0:T(8,128)(2,1)S(1)}, u32[]{:S(2)}, u32[]{:S(2)}) collective-permute-start(bf16[448,3328]{1,0:T(8,128)(2,1)} %constant_dynamic-slice_fusion.1), channel_id=1, source_target_pairs={{0,16},{16,0},{32,48},{48,32},{64,80},{80,64},{96,112},{112,96},{1... | collective-permute-start | bytes 8945672 | tf_op jit(solution)/shard_map/ppermute | solution.py:46
  4.8 19.9 %all-to-all-start = ((bf16[16,16,448]{2,0,1:T(8,128)(2,1)}), bf16[16,16,448]{2,0,1:T(8,128)(2,1)S(1)}, u32[]{:S(2)}, u32[]{:S(2)}) async-start(bf16[16,16,448]{2,0,1:T(8,128)(2,1)} %copy.85), calls=%async_computation | async-start | bytes 524288 | tf_op jit(solution)/shard_map/all_to_all | solution.py:54
  24.7 5.9 %collective-permute-start.1 = (bf16[256,448]{1,0:T(8,128)(2,1)S(1)}, bf16[256,448]{1,0:T(8,128)(2,1)S(1)}, u32[]{:S(2)}, u32[]{:S(2)}) collective-permute-start(bf16[256,448]{1,0:T(8,128)(2,1)S(1)} %bitcast.186), channel_id=1, source_target_pairs={{0,16},{16,0},{32,48},{48,32},{64,80},{80,64},{96,112},{112,96},{1... | collective-permute-start | bytes 688136 | tf_op jit(solution)/shard_map/ppermute | solution.py:46
  31.3 26.9 %copy-start = (f32[3328,128]{0,1:T(8,128)}, f32[3328,128]{0,1:T(8,128)S(1)}, u32[]{:S(2)}) copy-start(f32[3328,128]{0,1:T(8,128)S(1)} %convolution_add_fusion) | copy-start | bytes 5111812
  31.4 5.0 %collective-permute-start.24 = (f16[16,1664]{1,0:T(8,128)(2,1)S(1)}, f16[16,1664]{1,0:T(8,128)(2,1)S(1)}, u32[]{:S(2)}, u32[]{:S(2)}) collective-permute-start(f16[16,1664]{1,0:T(8,128)(2,1)S(1)} %get-tuple-element.50), channel_id=1, source_target_pairs={{0,224},{16,240},{32,0},{48,16},{64,32},{80,48},{96,64},{112,80},{... | collective-permute-start | bytes 159752 | tf_op jit(solution)/shard_map/ppermute | solution.py:48
  31.5 7.5 %collective-permute-start.20 = (f16[16,1664]{1,0:T(8,128)(2,1)S(1)}, f16[16,1664]{1,0:T(8,128)(2,1)S(1)}, u32[]{:S(2)}, u32[]{:S(2)}) collective-permute-start(f16[16,1664]{1,0:T(8,128)(2,1)S(1)} %get-tuple-element.49), channel_id=1, source_target_pairs={{0,32},{16,48},{32,64},{48,80},{64,96},{80,112},{96,128},{112,144}... | collective-permute-start | bytes 159752 | tf_op jit(solution)/shard_map/ppermute | solution.py:47
  33.5 28.7 %slice-start = ((s8[5963776]{0:T(1024)(128)(4,1)}), s8[4194304]{0:T(1024)(128)(4,1)S(1)}, s32[]{:S(2)}) async-start(s8[5963776]{0:T(1024)(128)(4,1)} %bitcast.184), calls=%async_computation.2 | async-start | bytes 8388608
  34.2 26.8 %copy-start.1 = (f32[3328,128]{0,1:T(8,128)}, f32[3328,128]{0,1:T(8,128)S(1)}, u32[]{:S(2)}) copy-start(f32[3328,128]{0,1:T(8,128)S(1)} %convolution_add_fusion.1) | copy-start | bytes 5111812
  34.2 28.0 %slice-start.1 = ((s8[5963776]{0:T(1024)(128)(4,1)}), s8[1769472]{0:T(1024)(128)(4,1)S(1)}, s32[]{:S(2)}) async-start(s8[5963776]{0:T(1024)(128)(4,1)} %bitcast.184), calls=%async_computation.3 | async-start | bytes 3538944
  34.3 4.9 %collective-permute-start.6 = (f16[16,1664]{1,0:T(8,128)(2,1)S(1)}, f16[16,1664]{1,0:T(8,128)(2,1)S(1)}, u32[]{:S(2)}, u32[]{:S(2)}) collective-permute-start(f16[16,1664]{1,0:T(8,128)(2,1)S(1)} %get-tuple-element.44), channel_id=1, source_target_pairs={{0,224},{16,240},{32,0},{48,16},{64,32},{80,48},{96,64},{112,80},{... | collective-permute-start | bytes 159752 | tf_op jit(solution)/shard_map/ppermute | solution.py:48
  35.7 6.9 %collective-permute-start.2 = (f16[16,1664]{1,0:T(8,128)(2,1)S(1)}, f16[16,1664]{1,0:T(8,128)(2,1)S(1)}, u32[]{:S(2)}, u32[]{:S(2)}) collective-permute-start(f16[16,1664]{1,0:T(8,128)(2,1)S(1)} %get-tuple-element.43), channel_id=1, source_target_pairs={{0,32},{16,48},{32,64},{48,80},{64,96},{80,112},{96,128},{112,144}... | collective-permute-start | bytes 159752 | tf_op jit(solution)/shard_map/ppermute | solution.py:47
  36.5 12.9 %collective-permute-start.25 = (f16[16,3328]{1,0:T(8,128)(2,1)S(1)}, f16[16,3328]{1,0:T(8,128)(2,1)S(1)}, u32[]{:S(2)}, u32[]{:S(2)}) collective-permute-start(f16[16,3328]{1,0:T(8,128)(2,1)S(1)} %fusion.37), channel_id=1, source_target_pairs={{0,224},{16,240},{32,0},{48,16},{64,32},{80,48},{96,64},{112,80},{... | collective-permute-start | bytes 319496 | tf_op jit(solution)/shard_map/ppermute | solution.py:48
  39.1 6.3 %collective-permute-start.21 = (f16[16,3328]{1,0:T(8,128)(2,1)S(1)}, f16[16,3328]{1,0:T(8,128)(2,1)S(1)}, u32[]{:S(2)}, u32[]{:S(2)}) collective-permute-start(f16[16,3328]{1,0:T(8,128)(2,1)S(1)} %fusion.36), channel_id=1, source_target_pairs={{0,32},{16,48},{32,64},{48,80},{64,96},{80,112},{96,128},{112,144}... | collective-permute-start | bytes 319496 | tf_op jit(solution)/shard_map/ppermute | solution.py:47
  39.3 15.4 %collective-permute-start.7 = (f16[16,3328]{1,0:T(8,128)(2,1)S(1)}, f16[16,3328]{1,0:T(8,128)(2,1)S(1)}, u32[]{:S(2)}, u32[]{:S(2)}) collective-permute-start(f16[16,3328]{1,0:T(8,128)(2,1)S(1)} %fusion.35), channel_id=1, source_target_pairs={{0,224},{16,240},{32,0},{48,16},{64,32},{80,48},{96,64},{112,80},{... | collective-permute-start | bytes 319496 | tf_op jit(solution)/shard_map/ppermute | solution.py:48
  42.6 6.4 %collective-permute-start.3 = (f16[16,3328]{1,0:T(8,128)(2,1)S(1)}, f16[16,3328]{1,0:T(8,128)(2,1)S(1)}, u32[]{:S(2)}, u32[]{:S(2)}) collective-permute-start(f16[16,3328]{1,0:T(8,128)(2,1)S(1)} %fusion.34), channel_id=1, source_target_pairs={{0,32},{16,48},{32,64},{48,80},{64,96},{80,112},{96,128},{112,144}... | collective-permute-start | bytes 319496 | tf_op jit(solution)/shard_map/ppermute | solution.py:47
  45.4 7.0 %collective-permute-start.22 = (f16[16,3328]{1,0:T(8,128)(2,1)S(1)}, f16[16,3328]{1,0:T(8,128)(2,1)S(1)}, u32[]{:S(2)}, u32[]{:S(2)}) collective-permute-start(f16[16,3328]{1,0:T(8,128)(2,1)S(1)} %fusion.43), channel_id=1, source_target_pairs={{0,32},{16,48},{32,64},{48,80},{64,96},{80,112},{96,128},{112,144}... | collective-permute-start | bytes 319496 | tf_op jit(solution)/shard_map/ppermute | solution.py:47
  49.1 6.2 %collective-permute-start.4 = (f16[16,3328]{1,0:T(8,128)(2,1)S(1)}, f16[16,3328]{1,0:T(8,128)(2,1)S(1)}, u32[]{:S(2)}, u32[]{:S(2)}) collective-permute-start(f16[16,3328]{1,0:T(8,128)(2,1)S(1)} %fusion.52), channel_id=1, source_target_pairs={{0,32},{16,48},{32,64},{48,80},{64,96},{80,112},{96,128},{112,144}... | collective-permute-start | bytes 319496 | tf_op jit(solution)/shard_map/ppermute | solution.py:47
  52.5 5.7 %collective-permute-start.26 = (f16[16,3328]{1,0:T(8,128)(2,1)S(1)}, f16[16,3328]{1,0:T(8,128)(2,1)S(1)}, u32[]{:S(2)}, u32[]{:S(2)}) collective-permute-start(f16[16,3328]{1,0:T(8,128)(2,1)S(1)} %get-tuple-element.29), channel_id=1, source_target_pairs={{0,224},{16,240},{32,0},{48,16},{64,32},{80,48},{96,64},{112,80},{... | collective-permute-start | bytes 319496 | tf_op jit(solution)/shard_map/ppermute | solution.py:48
  52.8 11.2 %collective-permute-start.23 = (f16[16,3328]{1,0:T(8,128)(2,1)S(1)}, f16[16,3328]{1,0:T(8,128)(2,1)S(1)}, u32[]{:S(2)}, u32[]{:S(2)}) collective-permute-start(f16[16,3328]{1,0:T(8,128)(2,1)S(1)} %get-tuple-element.28), channel_id=1, source_target_pairs={{0,32},{16,48},{32,64},{48,80},{64,96},{80,112},{96,128},{112,144}... | collective-permute-start | bytes 319496 | tf_op jit(solution)/shard_map/ppermute | solution.py:47
  55.4 5.6 %collective-permute-start.8 = (f16[16,3328]{1,0:T(8,128)(2,1)S(1)}, f16[16,3328]{1,0:T(8,128)(2,1)S(1)}, u32[]{:S(2)}, u32[]{:S(2)}) collective-permute-start(f16[16,3328]{1,0:T(8,128)(2,1)S(1)} %get-tuple-element.24), channel_id=1, source_target_pairs={{0,224},{16,240},{32,0},{48,16},{64,32},{80,48},{96,64},{112,80},{... | collective-permute-start | bytes 319496 | tf_op jit(solution)/shard_map/ppermute | solution.py:48
  56.2 7.8 %collective-permute-start.5 = (f16[16,3328]{1,0:T(8,128)(2,1)S(1)}, f16[16,3328]{1,0:T(8,128)(2,1)}, u32[]{:S(2)}, u32[]{:S(2)}) collective-permute-start(f16[16,3328]{1,0:T(8,128)(2,1)S(1)} %get-tuple-element.23), channel_id=1, source_target_pairs={{0,32},{16,48},{32,64},{48,80},{64,96},{80,112},{96,128},{112,144}... | collective-permute-start | bytes 319496 | tf_op jit(solution)/shard_map/ppermute | solution.py:47
  58.3 5.7 %collective-permute-start.27 = (f16[16,3328]{1,0:T(8,128)(2,1)S(1)}, f16[16,3328]{1,0:T(8,128)(2,1)}, u32[]{:S(2)}, u32[]{:S(2)}) collective-permute-start(f16[16,3328]{1,0:T(8,128)(2,1)S(1)} %fusion.41), channel_id=1, source_target_pairs={{0,224},{16,240},{32,0},{48,16},{64,32},{80,48},{96,64},{112,80},{... | collective-permute-start | bytes 319496 | tf_op jit(solution)/shard_map/ppermute | solution.py:48
  61.1 4.9 %collective-permute-start.9 = (f16[16,3328]{1,0:T(8,128)(2,1)S(1)}, f16[16,3328]{1,0:T(8,128)(2,1)}, u32[]{:S(2)}, u32[]{:S(2)}) collective-permute-start(f16[16,3328]{1,0:T(8,128)(2,1)S(1)} %fusion.50), channel_id=1, source_target_pairs={{0,224},{16,240},{32,0},{48,16},{64,32},{80,48},{96,64},{112,80},{... | collective-permute-start | bytes 319496 | tf_op jit(solution)/shard_map/ppermute | solution.py:48
  64.0 40.5 %collective-permute-start.18 = (bf16[3328,448]{0,1:T(8,128)(2,1)}, bf16[3328,448]{0,1:T(8,128)(2,1)S(1)}, u32[]{:S(2)}, u32[]{:S(2)}) collective-permute-start(bf16[3328,448]{0,1:T(8,128)(2,1)} %constant_dynamic-slice_fusion), channel_id=1, source_target_pairs={{0,16},{16,0},{32,48},{48,32},{64,80},{80,64},{96,112},{112,96},{1... | collective-permute-start | bytes 8945672 | tf_op jit(solution)/shard_map/ppermute | solution.py:46
  68.4 8.7 %collective-permute-start.10 = (bf16[16,3456]{1,0:T(8,128)(2,1)}, bf16[16,3456]{1,0:T(8,128)(2,1)}, u32[]{:S(2)}, u32[]{:S(2)}) collective-permute-start(bf16[16,3456]{1,0:T(8,128)(2,1)} %fusion.65), channel_id=1, source_target_pairs={{0,32},{16,48},{32,64},{48,80},{64,96},{80,112},{96,128},{112,144}... | collective-permute-start | bytes 331784 | tf_op jit(solution)/shard_map/ppermute | solution.py:47
  68.5 9.5 %collective-permute-start.11 = (bf16[16,3456]{1,0:T(8,128)(2,1)}, bf16[16,3456]{1,0:T(8,128)(2,1)S(1)}, u32[]{:S(2)}, u32[]{:S(2)}) collective-permute-start(bf16[16,3456]{1,0:T(8,128)(2,1)} %fusion.65), channel_id=1, source_target_pairs={{0,224},{16,240},{32,0},{48,16},{64,32},{80,48},{96,64},{112,80},{... | collective-permute-start | bytes 331784 | tf_op jit(solution)/shard_map/ppermute | solution.py:48
  72.0 9.3 %collective-permute-start.28 = (bf16[16,3456]{1,0:T(8,128)(2,1)S(1)}, bf16[16,3456]{1,0:T(8,128)(2,1)S(1)}, u32[]{:S(2)}, u32[]{:S(2)}) collective-permute-start(bf16[16,3456]{1,0:T(8,128)(2,1)S(1)} %fusion.66), channel_id=1, source_target_pairs={{0,32},{16,48},{32,64},{48,80},{64,96},{80,112},{96,128},{112,144}... | collective-permute-start | bytes 331784 | tf_op jit(solution)/shard_map/ppermute | solution.py:47
  72.1 10.0 %collective-permute-start.29 = (bf16[16,3456]{1,0:T(8,128)(2,1)S(1)}, bf16[16,3456]{1,0:T(8,128)(2,1)S(1)}, u32[]{:S(2)}, u32[]{:S(2)}) collective-permute-start(bf16[16,3456]{1,0:T(8,128)(2,1)S(1)} %fusion.66), channel_id=1, source_target_pairs={{0,224},{16,240},{32,0},{48,16},{64,32},{80,48},{96,64},{112,80},{... | collective-permute-start | bytes 331784 | tf_op jit(solution)/shard_map/ppermute | solution.py:48
  77.0 8.9 %collective-permute-start.12 = (bf16[16,3456]{1,0:T(8,128)(2,1)}, bf16[16,3456]{1,0:T(8,128)(2,1)S(1)}, u32[]{:S(2)}, u32[]{:S(2)}) collective-permute-start(bf16[16,3456]{1,0:T(8,128)(2,1)} %collective-permute-done.10), channel_id=1, source_target_pairs={{0,32},{16,48},{32,64},{48,80},{64,96},{80,112},{96,128},{112,144}... | collective-permute-start | bytes 331784 | tf_op jit(solution)/shard_map/ppermute | solution.py:47
  78.0 8.0 %collective-permute-start.13 = (bf16[16,3456]{1,0:T(8,128)(2,1)S(1)}, bf16[16,3456]{1,0:T(8,128)(2,1)S(1)}, u32[]{:S(2)}, u32[]{:S(2)}) collective-permute-start(bf16[16,3456]{1,0:T(8,128)(2,1)S(1)} %collective-permute-done.11), channel_id=1, source_target_pairs={{0,224},{16,240},{32,0},{48,16},{64,32},{80,48},{96,64},{112,80},{... | collective-permute-start | bytes 331784 | tf_op jit(solution)/shard_map/ppermute | solution.py:48
  81.3 8.0 %collective-permute-start.30 = (bf16[16,3456]{1,0:T(8,128)(2,1)S(1)}, bf16[16,3456]{1,0:T(8,128)(2,1)S(1)}, u32[]{:S(2)}, u32[]{:S(2)}) collective-permute-start(bf16[16,3456]{1,0:T(8,128)(2,1)S(1)} %collective-permute-done.28), channel_id=1, source_target_pairs={{0,32},{16,48},{32,64},{48,80},{64,96},{80,112},{96,128},{112,144}... | collective-permute-start | bytes 331784 | tf_op jit(solution)/shard_map/ppermute | solution.py:47
  82.1 8.0 %collective-permute-start.31 = (bf16[16,3456]{1,0:T(8,128)(2,1)S(1)}, bf16[16,3456]{1,0:T(8,128)(2,1)S(1)}, u32[]{:S(2)}, u32[]{:S(2)}) collective-permute-start(bf16[16,3456]{1,0:T(8,128)(2,1)S(1)} %collective-permute-done.29), channel_id=1, source_target_pairs={{0,224},{16,240},{32,0},{48,16},{64,32},{80,48},{96,64},{112,80},{... | collective-permute-start | bytes 331784 | tf_op jit(solution)/shard_map/ppermute | solution.py:48
  86.0 8.0 %collective-permute-start.14 = (bf16[16,3456]{1,0:T(8,128)(2,1)S(1)}, bf16[16,3456]{1,0:T(8,128)(2,1)S(1)}, u32[]{:S(2)}, u32[]{:S(2)}) collective-permute-start(bf16[16,3456]{1,0:T(8,128)(2,1)S(1)} %collective-permute-done.12), channel_id=1, source_target_pairs={{0,32},{16,48},{32,64},{48,80},{64,96},{80,112},{96,128},{112,144}... | collective-permute-start | bytes 331784 | tf_op jit(solution)/shard_map/ppermute | solution.py:47
  86.0 8.1 %collective-permute-start.15 = (bf16[16,3456]{1,0:T(8,128)(2,1)S(1)}, bf16[16,3456]{1,0:T(8,128)(2,1)S(1)}, u32[]{:S(2)}, u32[]{:S(2)}) collective-permute-start(bf16[16,3456]{1,0:T(8,128)(2,1)S(1)} %collective-permute-done.13), channel_id=1, source_target_pairs={{0,224},{16,240},{32,0},{48,16},{64,32},{80,48},{96,64},{112,80},{... | collective-permute-start | bytes 331784 | tf_op jit(solution)/shard_map/ppermute | solution.py:48
  89.3 8.0 %collective-permute-start.32 = (bf16[16,3456]{1,0:T(8,128)(2,1)S(1)}, bf16[16,3456]{1,0:T(8,128)(2,1)S(1)}, u32[]{:S(2)}, u32[]{:S(2)}) collective-permute-start(bf16[16,3456]{1,0:T(8,128)(2,1)S(1)} %collective-permute-done.30), channel_id=1, source_target_pairs={{0,32},{16,48},{32,64},{48,80},{64,96},{80,112},{96,128},{112,144}... | collective-permute-start | bytes 331784 | tf_op jit(solution)/shard_map/ppermute | solution.py:47
  90.1 7.4 %collective-permute-start.33 = (bf16[16,3456]{1,0:T(8,128)(2,1)S(1)}, bf16[16,3456]{1,0:T(8,128)(2,1)S(1)}, u32[]{:S(2)}, u32[]{:S(2)}) collective-permute-start(bf16[16,3456]{1,0:T(8,128)(2,1)S(1)} %collective-permute-done.31), channel_id=1, source_target_pairs={{0,224},{16,240},{32,0},{48,16},{64,32},{80,48},{96,64},{112,80},{... | collective-permute-start | bytes 331784 | tf_op jit(solution)/shard_map/ppermute | solution.py:48
  94.0 8.2 %collective-permute-start.16 = (bf16[16,1664]{1,0:T(8,128)(2,1)S(1)}, bf16[16,1664]{1,0:T(8,128)(2,1)S(1)}, u32[]{:S(2)}, u32[]{:S(2)}) collective-permute-start(bf16[16,1664]{1,0:T(8,128)(2,1)S(1)} %slice.248), channel_id=1, source_target_pairs={{0,32},{16,48},{32,64},{48,80},{64,96},{80,112},{96,128},{112,144}... | collective-permute-start | bytes 159752 | tf_op jit(solution)/shard_map/ppermute | solution.py:47
  94.1 9.4 %collective-permute-start.17 = (bf16[16,1792]{1,0:T(8,128)(2,1)S(1)}, bf16[16,1792]{1,0:T(8,128)(2,1)S(1)}, u32[]{:S(2)}, u32[]{:S(2)}) collective-permute-start(bf16[16,1792]{1,0:T(8,128)(2,1)S(1)} %slice.249), channel_id=1, source_target_pairs={{0,224},{16,240},{32,0},{48,16},{64,32},{80,48},{96,64},{112,80},{... | collective-permute-start | bytes 172040 | tf_op jit(solution)/shard_map/ppermute | solution.py:48
  97.4 5.4 %collective-permute-start.34 = (bf16[16,1664]{1,0:T(8,128)(2,1)S(1)}, bf16[16,1664]{1,0:T(8,128)(2,1)S(1)}, u32[]{:S(2)}, u32[]{:S(2)}) collective-permute-start(bf16[16,1664]{1,0:T(8,128)(2,1)S(1)} %slice.274), channel_id=1, source_target_pairs={{0,32},{16,48},{32,64},{48,80},{64,96},{80,112},{96,128},{112,144}... | collective-permute-start | bytes 159752 | tf_op jit(solution)/shard_map/ppermute | solution.py:47
  97.5 9.2 %collective-permute-start.35 = (bf16[16,1792]{1,0:T(8,128)(2,1)S(1)}, bf16[16,1792]{1,0:T(8,128)(2,1)S(1)}, u32[]{:S(2)}, u32[]{:S(2)}) collective-permute-start(bf16[16,1792]{1,0:T(8,128)(2,1)S(1)} %slice.275), channel_id=1, source_target_pairs={{0,224},{16,240},{32,0},{48,16},{64,32},{80,48},{96,64},{112,80},{... | collective-permute-start | bytes 172040 | tf_op jit(solution)/shard_map/ppermute | solution.py:48
  103.4 0.9 copy-start.2
  106.6 4.3 %collective-permute-start.19 = (bf16[128,512]{0,1:T(8,128)(2,1)S(1)}, bf16[128,512]{0,1:T(8,128)(2,1)S(1)}, u32[]{:S(2)}, u32[]{:S(2)}) collective-permute-start(bf16[128,512]{0,1:T(8,128)(2,1)S(1)} %pad_maximum_fusion.1), channel_id=1, source_target_pairs={{0,16},{16,0},{32,48},{48,32},{64,80},{80,64},{96,112},{112,96},{1... | collective-permute-start | bytes 393224 | tf_op jit(solution)/shard_map/ppermute | solution.py:46
  110.3 3.9 %collective-permute-start.36 = (bf16[128,512]{0,1:T(8,128)(2,1)S(1)}, bf16[128,512]{0,1:T(8,128)(2,1)S(1)}, u32[]{:S(2)}, u32[]{:S(2)}) collective-permute-start(bf16[128,512]{0,1:T(8,128)(2,1)S(1)} %pad_maximum_fusion.2), channel_id=1, source_target_pairs={{0,16},{16,0},{32,48},{48,32},{64,80},{80,64},{96,112},{112,96},{1... | collective-permute-start | bytes 393224 | tf_op jit(solution)/shard_map/ppermute | solution.py:46
  131.7 12.0 %collective-permute-start.37 = (bf16[16,448]{1,0:T(8,128)(2,1)S(1)}, bf16[16,448]{1,0:T(8,128)(2,1)S(1)}, u32[]{:S(2)}, u32[]{:S(2)}) collective-permute-start(bf16[16,448]{1,0:T(8,128)(2,1)S(1)} %divide_convert_fusion), channel_id=1, source_target_pairs={{0,0},{1,16},{2,32},{3,48},{4,64},{5,80},{6,96},{7,112},{8,128},{9... | collective-permute-start | bytes 43016 | tf_op jit(solution)/shard_map/ppermute | solution.py:119

commit v2 on v0

v2 whole, which is shorter than its diff:
```python
import jax
import jax.numpy as jnp
from jax import lax
from jax.sharding import PartitionSpec as P

WIRE = jnp.float16
SCALE = 1.0 / 64.0
BF16, F32 = jnp.bfloat16, jnp.float32
STAT = 128


def pieces(value):
    parts = []
    for _ in range(3):
        head = lax.reduce_precision(value, 8, 7)
        parts.append(head.astype(BF16))
        value = value - head
    return parts


def stat_block(top, total):
    block = jnp.concatenate(pieces(top) + pieces(total), -1)
    return jnp.pad(block, [(0, 0)] * (block.ndim - 1) + [(0, STAT - 6)])


def read_stats(block):
    block = block.astype(F32)
    top = block[..., 0:1] + block[..., 1:2] + block[..., 2:3]
    total = block[..., 3:4] + block[..., 4:5] + block[..., 5:6]
    return top, total


def on_device(hidden, head_table, embed_table):
    me = lax.axis_index("dp")
    z, core = me // 2, me % 2
    size = lax.axis_size("dp")
    chips = size // 2
    rows_dev = hidden.shape[0]
    feats, vocab = head_table.shape
    cut = (vocab // 256) * 128

    swap = lambda x: lax.ppermute(x, "dp", [(i, i ^ 1) for i in range(size)])
    up = lambda x: lax.ppermute(x, "dp", [(i, (i + 2) % size) for i in range(size)])
    down = lambda x: lax.ppermute(x, "dp", [(i, (i - 2) % size) for i in range(size)])
    dot = lambda a, b: jnp.dot(a, b, preferred_element_type=F32)
    enc = lambda x: (x * SCALE).astype(WIRE)
    dec = lambda x: x.astype(F32) * (1.0 / SCALE)

    groups = [[c + 2 * k for k in range(chips)] for c in range(2)]
    slices = lax.all_to_all(
        hidden, "dp", split_axis=1, concat_axis=0, tiled=True, axis_index_groups=groups
    )
    head_other = swap(head_table)
    embed_other = swap(embed_table)
    slices = jnp.roll(slices.reshape(chips, rows_dev, 2 * feats), -z, 0)
    first, second = slices[:, :, :feats], slices[:, :, feats:]
    own = jnp.where(core == 0, first, second).reshape(chips * rows_dev, feats)
    others = jnp.where(core == 0, second, first).reshape(chips * rows_dev, feats)

    logits = dot(own, head_table) + dot(others, head_other)
    logits = logits.reshape(chips, rows_dev, vocab)
    part = lambda o: logits[o % chips]

    far = part(4)
    a, b = up(enc(far[:, :cut])), down(enc(far[:, cut:]))
    p3, m3 = part(3), part(-3)
    a = up(enc(jnp.concatenate([p3[:, :cut] + dec(a), p3[:, cut:]], 1)))
    b = down(enc(jnp.concatenate([m3[:, :cut], m3[:, cut:] + dec(b)], 1)))
    a, b = up(enc(part(2) + dec(a))), down(enc(part(-2) + dec(b)))
    a, b = up(enc(part(1) + dec(a))), down(enc(part(-1) + dec(b)))
    full = part(0) + dec(a) + dec(b)

    top = jnp.max(full, axis=1, keepdims=True)
    scaled = jnp.exp(full - top)
    total = jnp.sum(scaled, axis=1, keepdims=True)
    block = jnp.concatenate([scaled.astype(BF16), stat_block(top, total)], 1)

    got = {0: block}
    a, b = block, block
    for step in range(1, 4):
        a, b = up(a), down(b)
        got[chips - step], got[step] = a, b
    a, b = up(a[:, :cut]), down(b[:, cut:])
    got[4] = jnp.concatenate([a, b], 1)

    def mix(order):
        block = jnp.concatenate([got[o] for o in order], 0)
        weights, stats = block[:, :vocab], block[:, vocab:]
        return dot(weights, embed_table).astype(BF16), dot(weights, embed_other).astype(BF16), stats

    early = mix([6, 7, 0, 1, 2])
    late = mix([3, 4, 5])
    value_own, value_other, stats = [jnp.concatenate([e, l], 0) for e, l in zip(early, late)]
    first = jnp.where(core == 0, value_own, value_other)
    second = jnp.where(core == 0, value_other, value_own)
    shape = lambda x: x.reshape(chips, rows_dev, x.shape[-1])
    first, second, stats = shape(first), shape(second), shape(stats)
    blocks = jnp.stack(
        [jnp.concatenate([first, stats], 2), jnp.concatenate([second, stats], 2)], 1
    )
    blocks = jnp.roll(blocks, z - 2, 0).reshape(size, rows_dev, feats + STAT)

    got = lax.all_to_all(blocks, "vocab", 0, 0)
    tops, tots = read_stats(got[:, :, feats:])
    factor = jnp.exp(tops - jnp.max(tops, axis=0, keepdims=True))
    row_total = jnp.sum(tots * factor, axis=0)
    mixture = jnp.sum(got[:, :, :feats].astype(F32) * factor, axis=0)
    result = (mixture / row_total).astype(BF16)
    flip = []
    for k in range(chips):
        for c in range(2):
            for r in range(chips):
                for f in range(2):
                    here = (2 * k + c) * size + 2 * r + f
                    there = (2 * r + c) * size + 2 * k + f
                    flip.append((here, there))
    return lax.ppermute(result, ("dp", "vocab"), flip)


def solution(mesh):
    in_specs = (P("dp", None), P("dp", "vocab"), P("vocab", "dp"))
    out_specs = P("dp", "vocab")
    return jax.shard_map(
        on_device, mesh=mesh, in_specs=in_specs, out_specs=out_specs, check_vma=False
    )
```

time: 313 us -> 136 us (0.43)
  waiting for transfers between devices: 183 us -> 58.1 us
  blocking collectives: 83.6 us -> 13.5 us
  starting transfers between devices: 5.47 us -> 32.6 us
  between operations: 13.4 us -> 0.29 us
  matrix products: 13.9 us -> 25.6 us
  other arithmetic: 8.03 us -> 2.54 us
    psum x1 -> x0, waiting for transfers between devices: 128 us -> none  [on_device(): lax.psum(jnp.dot(slices, head_table, preferred_element_type=jnp.float32),...]
    ppermute x0 -> x19, waiting for transfers between devices: none -> 46.3 us  [the longest x8 27.1 us: on_device(): lax.ppermute(x, 'dp', [(i, (i - 2) % size) for i in range(size)])]
    unnamed x3 -> x0, waiting for transfers between devices: 43.7 us -> none
    pmax x1 -> x0, blocking collectives: 33.3 us -> none  [row_stats(): row_top = lax.pmax(local_top, 'vocab')]
    psum x1 -> x0, blocking collectives: 30.8 us -> none  [row_stats(): row_total = lax.psum(jnp.sum(scaled, axis=1, keepdims=True), 'vocab')]
    ppermute x0 -> x19, starting transfers between devices: none -> 24.1 us  [the longest x8 11.1 us: on_device(): lax.ppermute(x, 'dp', [(i, (i - 2) % size) for i in range(size)])]
    dot_general x2 -> x6, matrix products: 13.9 us -> 25.6 us  [on_device(): dot = lambda a, b: jnp.dot(a, b, preferred_element_type=F32)]
    all_to_all x1, blocking collectives: 19.5 us -> 13.5 us  [on_device(): got = lax.all_to_all(blocks, 'vocab', 0, 0)]
  transfers between devices with their start and end apart: 3 -> 20, of which waited for: 3 -> 12; matrix products, arithmetic and copies ran while one was open for 1% -> 12% of each run, Pallas kernels for 0% -> 0%
where the time goes in v2:
time: 136 us; the launch traced here: 135 us
  waiting for transfers between devices  58.1 us (43%)
  starting transfers between devices  32.6 us (24%)
  matrix products  25.6 us (19%)
  blocking collectives  13.5 us (10%)
  other arithmetic  2.54 us (2%)
  local copies, waits for them, and re-layouts  2.47 us (2%)
    ppermute x8, waiting for transfers between devices, on_device(): lax.ppermute(x, 'dp', [(i, (i - 2) % size) for i in range(size)])  27.1 us
    dot_general x6, matrix products, on_device(): dot = lambda a, b: jnp.dot(a, b, preferred_element_type=F32)  25.6 us
    all_to_all x1, blocking collectives, on_device(): got = lax.all_to_all(blocks, 'vocab', 0, 0)  13.5 us
    ppermute x8, waiting for transfers between devices, on_device(): lax.ppermute(x, 'dp', [(i, (i + 2) % size) for i in range(size)])  12.7 us
    all_to_all x1, waiting for transfers between devices, on_device(): lax.all_to_all(hidden, 'dp', split_axis=1, concat_axis=0, tiled=True, axi...  11.8 us
    ppermute x8, starting transfers between devices, on_device(): lax.ppermute(x, 'dp', [(i, (i - 2) % size) for i in range(size)])  11.1 us
    all_to_all x1, starting transfers between devices, on_device(): lax.all_to_all(hidden, 'dp', split_axis=1, concat_axis=0, tiled=True, axi...  8.47 us
    ppermute x8, starting transfers between devices, on_device(): lax.ppermute(x, 'dp', [(i, (i + 2) % size) for i in range(size)])  7.43 us
  transfers between devices with their start and end apart: 20, of which 12 were waited for; matrix products, arithmetic and copies ran while one was open for 12% of the time, Pallas kernels for 0%

profile of v2, /device:TPU:16, one launch (start us, length us, event | category | flops | bytes accessed | tf_op | source)
XLA Modules:
  0.0 135.1 jit_solution(3932573970561224309)
XLA Ops:
  0.0 1.6 %copy.18 = bf16[2,8,8,896]{3,2,0,1:T(8,128)(2,1)} copy(bf16[2,8,8,896]{3,2,1,0:T(8,128)(2,1)} %bitcast.43) | data formatting | bytes 458752 | tf_op jit(solution)/shard_map/all_to_all | solution.py:50
  1.6 8.5 %all-to-all-start = ((bf16[16,8,896]{2,0,1:T(8,128)(2,1)}), bf16[16,8,896]{2,0,1:T(8,128)(2,1)S(1)}, u32[]{:S(2)}, u32[]{:S(2)}) async-start(bf16[16,8,896]{2,0,1:T(8,128)(2,1)} %bitcast.36), calls=%async_computation | async-start | bytes 458752 | tf_op jit(solution)/shard_map/all_to_all | solution.py:50
  10.1 11.8 %all-to-all-done = bf16[16,8,896]{2,0,1:T(8,128)(2,1)S(1)} async-done(((bf16[16,8,896]{2,0,1:T(8,128)(2,1)}), bf16[16,8,896]{2,0,1:T(8,128)(2,1)S(1)}, u32[]{:S(2)}, u32[]{:S(2)}) %all-to-all-start) | async-done | bytes 229408 | tf_op jit(solution)/shard_map/all_to_all | solution.py:50
  21.9 0.1 fusion.21
  22.1 0.1 broadcast_select_fusion
  22.2 3.7 %fusion.37 = f32[128,6656]{1,0:T(8,128)S(1)} fusion(bf16[128,448]{1,0:T(8,128)(2,1)S(1)} %bitcast.40, bf16[448,6656]{1,0:T(8,128)(2,1)} %param.4), kind=kOutput, calls=%fused_computation.95 | convolution fusion | flops 763363328 | bytes 9486336 | tf_op jit(solution)/shard_map/dot_general | solution.py:45
  25.9 3.9 %convolution_add_fusion = f32[128,6656]{1,0:T(8,128)S(1)} fusion(f32[128,6656]{1,0:T(8,128)S(1)} %fusion.37, bf16[128,448]{1,0:T(8,128)(2,1)S(1)} %bitcast.39, bf16[448,6656]{1,0:T(8,128)(2,1)} %collective-permute-done), kind=kOutput, calls=%fused_computation | convolution fusion | flops 764215296 | bytes 12894208 | tf_op jit(solution)/shard_map/dot_general | solution.py:45
  29.8 0.6 collective-permute-start.1
  30.5 5.5 %collective-permute-done.1 = f16[16,3328]{1,0:T(8,128)(2,1)S(1)} collective-permute-done((f16[16,3328]{1,0:T(8,128)(2,1)S(1)}, f16[16,3328]{1,0:T(8,128)(2,1)S(1)}, u32[]{:S(2)}, u32[]{:S(2)}) %collective-permute-start.1) | collective-permute-done | bytes 106528 | tf_op jit(solution)/shard_map/ppermute | solution.py:43
  36.1 0.1 collective-permute-start.5
  36.2 2.1 %collective-permute-start.2 = (f16[16,6656]{1,0:T(8,128)(2,1)S(1)}, f16[16,6656]{1,0:T(8,128)(2,1)S(1)}, u32[]{:S(2)}, u32[]{:S(2)}) collective-permute-start(f16[16,6656]{1,0:T(8,128)(2,1)S(1)} %fusion.14), channel_id=1, source_target_pairs={{0,32},{16,48},{32,64},{48,80},{64,96},{80,112},{96,128},{112,144}... | collective-permute-start | bytes 638984 | tf_op jit(solution)/shard_map/ppermute | solution.py:43
  38.3 2.6 %collective-permute-done.5 = f16[16,3328]{1,0:T(8,128)(2,1)S(1)} collective-permute-done((f16[16,3328]{1,0:T(8,128)(2,1)S(1)}, f16[16,3328]{1,0:T(8,128)(2,1)S(1)}, u32[]{:S(2)}, u32[]{:S(2)}) %collective-permute-start.5) | collective-permute-done | bytes 106528 | tf_op jit(solution)/shard_map/ppermute | solution.py:44
  41.0 1.3 collective-permute-start.6
  42.3 1.6 %collective-permute-done.2 = f16[16,6656]{1,0:T(8,128)(2,1)S(1)} collective-permute-done((f16[16,6656]{1,0:T(8,128)(2,1)S(1)}, f16[16,6656]{1,0:T(8,128)(2,1)S(1)}, u32[]{:S(2)}, u32[]{:S(2)}) %collective-permute-start.2) | collective-permute-done | bytes 213024 | tf_op jit(solution)/shard_map/ppermute | solution.py:43
  43.9 0.6 collective-permute-start.3
  44.5 2.4 %collective-permute-done.6 = f16[16,6656]{1,0:T(8,128)(2,1)S(1)} collective-permute-done((f16[16,6656]{1,0:T(8,128)(2,1)S(1)}, f16[16,6656]{1,0:T(8,128)(2,1)S(1)}, u32[]{:S(2)}, u32[]{:S(2)}) %collective-permute-start.6) | collective-permute-done | bytes 213024 | tf_op jit(solution)/shard_map/ppermute | solution.py:44
  46.9 4.2 %collective-permute-done.3 = f16[16,6656]{1,0:T(8,128)(2,1)S(1)} collective-permute-done((f16[16,6656]{1,0:T(8,128)(2,1)S(1)}, f16[16,6656]{1,0:T(8,128)(2,1)S(1)}, u32[]{:S(2)}, u32[]{:S(2)}) %collective-permute-start.3) | collective-permute-done | bytes 213024 | tf_op jit(solution)/shard_map/ppermute | solution.py:43
  51.1 0.2 fusion.12
  51.2 0.1 collective-permute-start.7
  51.3 2.0 %collective-permute-start.4 = (f16[16,6656]{1,0:T(8,128)(2,1)S(1)}, f16[16,6656]{1,0:T(8,128)(2,1)S(1)}, u32[]{:S(2)}, u32[]{:S(2)}) collective-permute-start(f16[16,6656]{1,0:T(8,128)(2,1)S(1)} %get-tuple-element.11), channel_id=1, source_target_pairs={{0,32},{16,48},{32,64},{48,80},{64,96},{80,112},{96,128},{112,144}... | collective-permute-start | bytes 638984 | tf_op jit(solution)/shard_map/ppermute | solution.py:43
  53.4 5.1 %collective-permute-done.7 = f16[16,6656]{1,0:T(8,128)(2,1)S(1)} collective-permute-done((f16[16,6656]{1,0:T(8,128)(2,1)S(1)}, f16[16,6656]{1,0:T(8,128)(2,1)S(1)}, u32[]{:S(2)}, u32[]{:S(2)}) %collective-permute-start.7) | collective-permute-done | bytes 213024 | tf_op jit(solution)/shard_map/ppermute | solution.py:44
  58.6 0.1 collective-permute-start.8
  58.6 0.1 collective-permute-start.17
  58.8 7.5 %collective-permute-done.8 = f16[16,6656]{1,0:T(8,128)(2,1)S(1)} collective-permute-done((f16[16,6656]{1,0:T(8,128)(2,1)S(1)}, f16[16,6656]{1,0:T(8,128)(2,1)S(1)}, u32[]{:S(2)}, u32[]{:S(2)}) %collective-permute-start.8) | collective-permute-done | bytes 213024 | tf_op jit(solution)/shard_map/ppermute | solution.py:44
  66.3 0.2 fusion.35
  66.5 0.3 fusion.17
  66.8 0.1 copy.15
  67.0 2.0 %collective-permute-start.9 = (bf16[16,6784]{1,0:T(8,128)(2,1)S(1)}, bf16[16,6784]{1,0:T(8,128)(2,1)S(1)}, u32[]{:S(2)}, u32[]{:S(2)}) collective-permute-start(bf16[16,6784]{1,0:T(8,128)(2,1)S(1)} %fusion.22), channel_id=1, source_target_pairs={{0,32},{16,48},{32,64},{48,80},{64,96},{80,112},{96,128},{112,144}... | collective-permute-start | bytes 651272 | tf_op jit(solution)/shard_map/ppermute | solution.py:43
  69.0 4.9 %collective-permute-done.11 = bf16[16,6784]{1,0:T(8,128)(2,1)S(1)} collective-permute-done((bf16[16,6784]{1,0:T(8,128)(2,1)S(1)}, bf16[16,6784]{1,0:T(8,128)(2,1)S(1)}, u32[]{:S(2)}, u32[]{:S(2)}) %collective-permute-start.11) | collective-permute-done | bytes 217120 | tf_op jit(solution)/shard_map/ppermute | solution.py:44
  73.9 2.4 %collective-permute-start.12 = (bf16[16,6784]{1,0:T(8,128)(2,1)S(1)}, bf16[16,6784]{1,0:T(8,128)(2,1)S(1)}, u32[]{:S(2)}, u32[]{:S(2)}) collective-permute-start(bf16[16,6784]{1,0:T(8,128)(2,1)S(1)} %collective-permute-done.11), channel_id=1, source_target_pairs={{0,224},{16,240},{32,0},{48,16},{64,32},{80,48},{96,64},{112,80},{... | collective-permute-start | bytes 651272 | tf_op jit(solution)/shard_map/ppermute | solution.py:44
  76.3 4.8 %collective-permute-done.12 = bf16[16,6784]{1,0:T(8,128)(2,1)S(1)} collective-permute-done((bf16[16,6784]{1,0:T(8,128)(2,1)S(1)}, bf16[16,6784]{1,0:T(8,128)(2,1)S(1)}, u32[]{:S(2)}, u32[]{:S(2)}) %collective-permute-start.12) | collective-permute-done | bytes 217120 | tf_op jit(solution)/shard_map/ppermute | solution.py:44
  81.1 3.7 %collective-permute-start.13 = (bf16[16,6784]{1,0:T(8,128)(2,1)S(1)}, bf16[16,6784]{1,0:T(8,128)(2,1)S(1)}, u32[]{:S(2)}, u32[]{:S(2)}) collective-permute-start(bf16[16,6784]{1,0:T(8,128)(2,1)S(1)} %collective-permute-done.12), channel_id=1, source_target_pairs={{0,224},{16,240},{32,0},{48,16},{64,32},{80,48},{96,64},{112,80},{... | collective-permute-start | bytes 651272 | tf_op jit(solution)/shard_map/ppermute | solution.py:44
  84.9 4.5 %convolution_convert_fusion.1 = bf16[80,448]{1,0:T(8,128)(2,1)S(1)} fusion(bf16[6656,448]{0,1:T(8,128)(2,1)} %param.5, bf16[80,6784]{1,0:T(8,128)(2,1)S(1)} %constant_dynamic-update-slice_fusion), kind=kOutput, calls=%fused_computation.2 | convolution fusion | flops 477137920 | bytes 7100416 | tf_op jit(solution)/shard_map/dot_general | solution.py:45
  89.4 3.3 %collective-permute-start.16 = (bf16[16,3456]{1,0:T(8,128)(2,1)S(1)}, bf16[16,3456]{1,0:T(8,128)(2,1)S(1)}, u32[]{:S(2)}, u32[]{:S(2)}) collective-permute-start(bf16[16,3456]{1,0:T(8,128)(2,1)S(1)} %slice.140), channel_id=1, source_target_pairs={{0,224},{16,240},{32,0},{48,16},{64,32},{80,48},{96,64},{112,80},{... | collective-permute-start | bytes 331784 | tf_op jit(solution)/shard_map/ppermute | solution.py:44
  92.9 4.5 %convolution_convert_fusion = bf16[80,448]{1,0:T(8,128)(2,1)S(1)} fusion(bf16[6656,448]{0,1:T(8,128)(2,1)} %collective-permute-done.17, bf16[80,6784]{1,0:T(8,128)(2,1)S(1)} %constant_dynamic-update-slice_fusion), kind=kOutput, calls=%fused_computation.1 | convolution fusion | flops 477137920 | bytes 7100416 | tf_op jit(solution)/shard_map/dot_general | solution.py:45
  97.4 1.4 %collective-permute-done.15 = bf16[16,3328]{1,0:T(8,128)(2,1)S(1)} collective-permute-done((bf16[16,3328]{1,0:T(8,128)(2,1)S(1)}, bf16[16,3328]{1,0:T(8,128)(2,1)S(1)}, u32[]{:S(2)}, u32[]{:S(2)}) %collective-permute-start.15) | collective-permute-done | bytes 106528 | tf_op jit(solution)/shard_map/ppermute | solution.py:43
  98.8 4.4 %convolution_convert_fusion.3 = bf16[48,448]{1,0:T(8,128)(2,1)S(1)} fusion(bf16[6656,448]{0,1:T(8,128)(2,1)} %param.5, bf16[48,6784]{1,0:T(8,128)(2,1)S(1)} %pad_maximum_fusion), kind=kOutput, calls=%fused_computation.4 | convolution fusion | flops 286282752 | bytes 6645760 | tf_op jit(solution)/shard_map/dot_general | solution.py:45
  103.3 4.4 %convolution_convert_fusion.2 = bf16[48,448]{1,0:T(8,128)(2,1)S(1)} fusion(bf16[6656,448]{0,1:T(8,128)(2,1)} %collective-permute-done.17, bf16[48,6784]{1,0:T(8,128)(2,1)S(1)} %pad_maximum_fusion), kind=kOutput, calls=%fused_computation.3 | convolution fusion | flops 286282752 | bytes 6645760 | tf_op jit(solution)/shard_map/dot_general | solution.py:45
  107.8 0.1 fusion.26
  107.9 0.2 fusion.19
  108.1 13.5 %all_to_all.21 = bf16[16,16,576]{2,1,0:T(8,128)(2,1)S(1)} all-to-all(bf16[16,16,576]{2,1,0:T(8,128)(2,1)S(1)} %bitcast.37), channel_id=1, replica_groups=mesh['dp'=16,'vocab'=16] {'vocab'}, dimensions={0} | all-to-all | bytes 589824 | tf_op jit(solution)/shard_map/all_to_all | solution.py:103
  121.6 0.1 slice_convert_fusion
  121.7 0.2 fusion.36
  122.0 0.3 fusion.28
  122.3 0.1 multiply_reduce_fusion
  122.5 5.5 %collective-permute-start.18 = (bf16[16,448]{1,0:T(8,128)(2,1)S(1)}, bf16[16,448]{1,0:T(8,128)(2,1)S(1)}, u32[]{:S(2)}, u32[]{:S(2)}) collective-permute-start(bf16[16,448]{1,0:T(8,128)(2,1)S(1)} %divide_convert_fusion), channel_id=1, source_target_pairs={{0,0},{1,1},{2,32},{3,33},{4,64},{5,65},{6,96},{7,97},{8,128},{9,1... | collective-permute-start | bytes 43016 | tf_op jit(solution)/shard_map/ppermute | solution.py:117
  128.1 6.5 %collective-permute-done.18 = bf16[16,448]{1,0:T(8,128)(2,1)S(1)} collective-permute-done((bf16[16,448]{1,0:T(8,128)(2,1)S(1)}, bf16[16,448]{1,0:T(8,128)(2,1)S(1)}, u32[]{:S(2)}, u32[]{:S(2)}) %collective-permute-start.18) | collective-permute-done | bytes 14368 | tf_op jit(solution)/shard_map/ppermute | solution.py:117
  134.5 0.6 copy.24
  (35 shorter events, 0.9 us)
Async XLA Ops:
  0.0 25.9 %collective-permute-start = (bf16[448,6656]{1,0:T(8,128)(2,1)}, bf16[448,6656]{1,0:T(8,128)(2,1)}, u32[]{:S(2)}, u32[]{:S(2)}) collective-permute-start(bf16[448,6656]{1,0:T(8,128)(2,1)} %param.4), channel_id=1, source_target_pairs={{0,16},{16,0},{32,48},{48,32},{64,80},{80,64},{96,112},{112,96},{1... | collective-permute-start | bytes 17891336 | tf_op jit(solution)/shard_map/ppermute | solution.py:42
  1.6 20.3 %all-to-all-start = ((bf16[16,8,896]{2,0,1:T(8,128)(2,1)}), bf16[16,8,896]{2,0,1:T(8,128)(2,1)S(1)}, u32[]{:S(2)}, u32[]{:S(2)}) async-start(bf16[16,8,896]{2,0,1:T(8,128)(2,1)} %bitcast.36), calls=%async_computation | async-start | bytes 458752 | tf_op jit(solution)/shard_map/all_to_all | solution.py:50
  29.8 6.2 %collective-permute-start.1 = (f16[16,3328]{1,0:T(8,128)(2,1)S(1)}, f16[16,3328]{1,0:T(8,128)(2,1)S(1)}, u32[]{:S(2)}, u32[]{:S(2)}) collective-permute-start(f16[16,3328]{1,0:T(8,128)(2,1)S(1)} %fusion.24), channel_id=1, source_target_pairs={{0,32},{16,48},{32,64},{48,80},{64,96},{80,112},{96,128},{112,144}... | collective-permute-start | bytes 319496 | tf_op jit(solution)/shard_map/ppermute | solution.py:43
  36.1 4.8 %collective-permute-start.5 = (f16[16,3328]{1,0:T(8,128)(2,1)S(1)}, f16[16,3328]{1,0:T(8,128)(2,1)S(1)}, u32[]{:S(2)}, u32[]{:S(2)}) collective-permute-start(f16[16,3328]{1,0:T(8,128)(2,1)S(1)} %get-tuple-element.14), channel_id=1, source_target_pairs={{0,224},{16,240},{32,0},{48,16},{64,32},{80,48},{96,64},{112,80},{... | collective-permute-start | bytes 319496 | tf_op jit(solution)/shard_map/ppermute | solution.py:44
  36.2 7.6 %collective-permute-start.2 = (f16[16,6656]{1,0:T(8,128)(2,1)S(1)}, f16[16,6656]{1,0:T(8,128)(2,1)S(1)}, u32[]{:S(2)}, u32[]{:S(2)}) collective-permute-start(f16[16,6656]{1,0:T(8,128)(2,1)S(1)} %fusion.14), channel_id=1, source_target_pairs={{0,32},{16,48},{32,64},{48,80},{64,96},{80,112},{96,128},{112,144}... | collective-permute-start | bytes 638984 | tf_op jit(solution)/shard_map/ppermute | solution.py:43
  41.0 5.9 %collective-permute-start.6 = (f16[16,6656]{1,0:T(8,128)(2,1)S(1)}, f16[16,6656]{1,0:T(8,128)(2,1)S(1)}, u32[]{:S(2)}, u32[]{:S(2)}) collective-permute-start(f16[16,6656]{1,0:T(8,128)(2,1)S(1)} %fusion.15), channel_id=1, source_target_pairs={{0,224},{16,240},{32,0},{48,16},{64,32},{80,48},{96,64},{112,80},{... | collective-permute-start | bytes 638984 | tf_op jit(solution)/shard_map/ppermute | solution.py:44
  43.9 7.1 %collective-permute-start.3 = (f16[16,6656]{1,0:T(8,128)(2,1)S(1)}, f16[16,6656]{1,0:T(8,128)(2,1)S(1)}, u32[]{:S(2)}, u32[]{:S(2)}) collective-permute-start(f16[16,6656]{1,0:T(8,128)(2,1)S(1)} %fusion.10), channel_id=1, source_target_pairs={{0,32},{16,48},{32,64},{48,80},{64,96},{80,112},{96,128},{112,144}... | collective-permute-start | bytes 638984 | tf_op jit(solution)/shard_map/ppermute | solution.py:43
  51.2 7.2 %collective-permute-start.7 = (f16[16,6656]{1,0:T(8,128)(2,1)S(1)}, f16[16,6656]{1,0:T(8,128)(2,1)S(1)}, u32[]{:S(2)}, u32[]{:S(2)}) collective-permute-start(f16[16,6656]{1,0:T(8,128)(2,1)S(1)} %get-tuple-element.12), channel_id=1, source_target_pairs={{0,224},{16,240},{32,0},{48,16},{64,32},{80,48},{96,64},{112,80},{... | collective-permute-start | bytes 638984 | tf_op jit(solution)/shard_map/ppermute | solution.py:44
  51.3 7.4 %collective-permute-start.4 = (f16[16,6656]{1,0:T(8,128)(2,1)S(1)}, f16[16,6656]{1,0:T(8,128)(2,1)S(1)}, u32[]{:S(2)}, u32[]{:S(2)}) collective-permute-start(f16[16,6656]{1,0:T(8,128)(2,1)S(1)} %get-tuple-element.11), channel_id=1, source_target_pairs={{0,32},{16,48},{32,64},{48,80},{64,96},{80,112},{96,128},{112,144}... | collective-permute-start | bytes 638984 | tf_op jit(solution)/shard_map/ppermute | solution.py:43
  58.6 7.7 %collective-permute-start.8 = (f16[16,6656]{1,0:T(8,128)(2,1)S(1)}, f16[16,6656]{1,0:T(8,128)(2,1)S(1)}, u32[]{:S(2)}, u32[]{:S(2)}) collective-permute-start(f16[16,6656]{1,0:T(8,128)(2,1)S(1)} %fusion.8), channel_id=1, source_target_pairs={{0,224},{16,240},{32,0},{48,16},{64,32},{80,48},{96,64},{112,80},{... | collective-permute-start | bytes 638984 | tf_op jit(solution)/shard_map/ppermute | solution.py:44
  58.6 34.2 %collective-permute-start.17 = (bf16[6656,448]{0,1:T(8,128)(2,1)}, bf16[6656,448]{0,1:T(8,128)(2,1)}, u32[]{:S(2)}, u32[]{:S(2)}) collective-permute-start(bf16[6656,448]{0,1:T(8,128)(2,1)} %param.5), channel_id=1, source_target_pairs={{0,16},{16,0},{32,48},{48,32},{64,80},{80,64},{96,112},{112,96},{1... | collective-permute-start | bytes 17891336 | tf_op jit(solution)/shard_map/ppermute | solution.py:42
  66.9 7.0 %collective-permute-start.11 = (bf16[16,6784]{1,0:T(8,128)(2,1)S(1)}, bf16[16,6784]{1,0:T(8,128)(2,1)S(1)}, u32[]{:S(2)}, u32[]{:S(2)}) collective-permute-start(bf16[16,6784]{1,0:T(8,128)(2,1)S(1)} %fusion.22), channel_id=1, source_target_pairs={{0,224},{16,240},{32,0},{48,16},{64,32},{80,48},{96,64},{112,80},{... | collective-permute-start | bytes 651272 | tf_op jit(solution)/shard_map/ppermute | solution.py:44
  67.0 9.3 %collective-permute-start.9 = (bf16[16,6784]{1,0:T(8,128)(2,1)S(1)}, bf16[16,6784]{1,0:T(8,128)(2,1)S(1)}, u32[]{:S(2)}, u32[]{:S(2)}) collective-permute-start(bf16[16,6784]{1,0:T(8,128)(2,1)S(1)} %fusion.22), channel_id=1, source_target_pairs={{0,32},{16,48},{32,64},{48,80},{64,96},{80,112},{96,128},{112,144}... | collective-permute-start | bytes 651272 | tf_op jit(solution)/shard_map/ppermute | solution.py:43
  73.9 7.2 %collective-permute-start.12 = (bf16[16,6784]{1,0:T(8,128)(2,1)S(1)}, bf16[16,6784]{1,0:T(8,128)(2,1)S(1)}, u32[]{:S(2)}, u32[]{:S(2)}) collective-permute-start(bf16[16,6784]{1,0:T(8,128)(2,1)S(1)} %collective-permute-done.11), channel_id=1, source_target_pairs={{0,224},{16,240},{32,0},{48,16},{64,32},{80,48},{96,64},{112,80},{... | collective-permute-start | bytes 651272 | tf_op jit(solution)/shard_map/ppermute | solution.py:44
  76.3 8.4 %collective-permute-start.10 = (bf16[16,6784]{1,0:T(8,128)(2,1)S(1)}, bf16[16,6784]{1,0:T(8,128)(2,1)S(1)}, u32[]{:S(2)}, u32[]{:S(2)}) collective-permute-start(bf16[16,6784]{1,0:T(8,128)(2,1)S(1)} %collective-permute-done.9), channel_id=1, source_target_pairs={{0,32},{16,48},{32,64},{48,80},{64,96},{80,112},{96,128},{112,144}... | collective-permute-start | bytes 651272 | tf_op jit(solution)/shard_map/ppermute | solution.py:43
  81.1 8.4 %collective-permute-start.13 = (bf16[16,6784]{1,0:T(8,128)(2,1)S(1)}, bf16[16,6784]{1,0:T(8,128)(2,1)S(1)}, u32[]{:S(2)}, u32[]{:S(2)}) collective-permute-start(bf16[16,6784]{1,0:T(8,128)(2,1)S(1)} %collective-permute-done.12), channel_id=1, source_target_pairs={{0,224},{16,240},{32,0},{48,16},{64,32},{80,48},{96,64},{112,80},{... | collective-permute-start | bytes 651272 | tf_op jit(solution)/shard_map/ppermute | solution.py:44
  84.8 8.0 %collective-permute-start.14 = (bf16[16,6784]{1,0:T(8,128)(2,1)S(1)}, bf16[16,6784]{1,0:T(8,128)(2,1)S(1)}, u32[]{:S(2)}, u32[]{:S(2)}) collective-permute-start(bf16[16,6784]{1,0:T(8,128)(2,1)S(1)} %collective-permute-done.10), channel_id=1, source_target_pairs={{0,32},{16,48},{32,64},{48,80},{64,96},{80,112},{96,128},{112,144}... | collective-permute-start | bytes 651272 | tf_op jit(solution)/shard_map/ppermute | solution.py:43
  89.4 9.3 %collective-permute-start.16 = (bf16[16,3456]{1,0:T(8,128)(2,1)S(1)}, bf16[16,3456]{1,0:T(8,128)(2,1)S(1)}, u32[]{:S(2)}, u32[]{:S(2)}) collective-permute-start(bf16[16,3456]{1,0:T(8,128)(2,1)S(1)} %slice.140), channel_id=1, source_target_pairs={{0,224},{16,240},{32,0},{48,16},{64,32},{80,48},{96,64},{112,80},{... | collective-permute-start | bytes 331784 | tf_op jit(solution)/shard_map/ppermute | solution.py:44
  92.8 6.0 %collective-permute-start.15 = (bf16[16,3328]{1,0:T(8,128)(2,1)S(1)}, bf16[16,3328]{1,0:T(8,128)(2,1)S(1)}, u32[]{:S(2)}, u32[]{:S(2)}) collective-permute-start(bf16[16,3328]{1,0:T(8,128)(2,1)S(1)} %slice.139), channel_id=1, source_target_pairs={{0,32},{16,48},{32,64},{48,80},{64,96},{80,112},{96,128},{112,144}... | collective-permute-start | bytes 319496 | tf_op jit(solution)/shard_map/ppermute | solution.py:43
  122.5 12.0 %collective-permute-start.18 = (bf16[16,448]{1,0:T(8,128)(2,1)S(1)}, bf16[16,448]{1,0:T(8,128)(2,1)S(1)}, u32[]{:S(2)}, u32[]{:S(2)}) collective-permute-start(bf16[16,448]{1,0:T(8,128)(2,1)S(1)} %divide_convert_fusion), channel_id=1, source_target_pairs={{0,0},{1,1},{2,32},{3,33},{4,64},{5,65},{6,96},{7,97},{8,128},{9,1... | collective-permute-start | bytes 43016 | tf_op jit(solution)/shard_map/ppermute | solution.py:117

commit v3 on v0

v3 whole, which is shorter than its diff:
```python
import jax
import jax.numpy as jnp
from jax import lax
from jax.experimental import pallas as pl
from jax.experimental.pallas import tpu as pltpu
from jax.sharding import PartitionSpec as P

BF16, F32 = jnp.bfloat16, jnp.float32
WIRE = jnp.float16
SCALE = 1.0 / 64.0
TILE, HALF = 128, 64
LOW = -3.0e38
PLACE = [7, 2, 11, 6, 3, 14, 12, 13, 0, 1, 4, 5, 15, 9, 8, 10]


def place(z, r, f):
    rel = PLACE[2 * ((r - z) % 8) + f]
    return (z // 2 + rel // 4) % 4 * 4 + (2 * z + rel) % 4

VMEM = pl.BlockSpec(memory_space=pltpu.VMEM)
HBM = pl.BlockSpec(memory_space=pltpu.HBM)
stay = lambda x: pltpu.with_memory_space_constraint(x, pltpu.HBM)
limit = pltpu.CompilerParams(vmem_limit_bytes=16 << 20)
iota = lambda rows: lax.broadcasted_iota(jnp.int32, (rows, TILE), 1)


def here():
    me = lax.axis_index("dp")
    return me >> 1, me & 1


def chunk_of(d):
    z, core = here()
    return (z + (1 - 2 * core) * d) & 7


def window(d, width):
    chunk, half = chunk_of(d), width // TILE - 1
    start = ((2 * half + 1) * (chunk >> 1) + half * (chunk & 1)) * TILE
    return pl.ds(pl.multiple_of(start, TILE), width)


def cost(flops, size):
    return pl.CostEstimate(flops=flops, bytes_accessed=size, transcendentals=0)


def pieces(value):
    parts = []
    for _ in range(3):
        head = value.astype(BF16)
        parts.append(head)
        value = value - head.astype(F32)
    return parts


def stat_lanes(top, total, rows):
    lane = iota(rows) % HALF
    out = jnp.zeros((rows, TILE), F32)
    for i, piece in enumerate(pieces(top) + pieces(total)):
        out = jnp.where(lane == i, piece.astype(F32), out)
    return out


def read_lanes(tile, lane):
    top = jnp.sum(jnp.where((lane >= 0) & (lane < 3), tile, 0.0), axis=-1, keepdims=True)
    total = jnp.sum(jnp.where((lane >= 3) & (lane < 6), tile, 0.0), axis=-1, keepdims=True)
    return top, total


def deal_kernel(hidden_ref, out_ref, sem):
    width = out_ref.shape[2]
    copies = [
        pltpu.make_async_copy(hidden_ref.at[:, k * width : (k + 1) * width], out_ref.at[k], sem.at[k])
        for k in range(out_ref.shape[0])
    ]
    for copy in copies:
        copy.start()
    for copy in copies:
        copy.wait()


def deal(hidden, parts):
    rows, feats = hidden.shape
    return pl.pallas_call(
        deal_kernel,
        out_shape=jax.ShapeDtypeStruct((parts, rows, feats // parts), BF16),
        in_specs=[HBM],
        out_specs=VMEM,
        scratch_shapes=[pltpu.SemaphoreType.DMA((parts,))],
        cost_estimate=cost(0, 1 << 19),
        compiler_params=limit,
        name="deal",
    )(stay(hidden))


def logits_kernel(order, own_ref, other_ref, *refs):
    tables, outs, (buf, sem) = refs[:2], refs[2:-2], refs[-2:]
    width = outs[0].shape[1]
    copies = [
        [
            pltpu.make_async_copy(t.at[:, window(d, width)], buf.at[slot, k], sem.at[slot, k])
            for k, t in enumerate(tables)
        ]
        for slot, d in enumerate(order)
    ]
    for pair in copies:
        for copy in pair:
            copy.start()
    for slot in range(len(order)):
        copies[slot][0].wait()
        part = jnp.dot(own_ref[...], buf[slot, 0], preferred_element_type=F32)
        copies[slot][1].wait()
        outs[slot][...] = part + jnp.dot(other_ref[...], buf[slot, 1], preferred_element_type=F32)


def logits_of(order, own, other, tables, width):
    rows, feats = own.shape
    n = len(order)
    return pl.pallas_call(
        lambda *refs: logits_kernel(order, *refs),
        out_shape=[jax.ShapeDtypeStruct((rows, width), F32)] * n,
        in_specs=[VMEM] * 2 + [HBM] * 2,
        out_specs=[VMEM] * n,
        scratch_shapes=[
            pltpu.VMEM((n, 2, feats, width), BF16),
            pltpu.SemaphoreType.DMA((n, 2)),
        ],
        cost_estimate=cost(4 * n * rows * feats * width, 4 * n * feats * width),
        compiler_params=limit,
        name=f"logits{n}",
    )(own, other, *[stay(t) for t in tables])


def softmax_kernel(full_ref, unused_ref, out_ref):
    rows, width = full_ref.shape
    odd = (chunk_of(0) & 1) == 1
    last = width - TILE
    lane = iota(rows)
    mine0 = jnp.logical_or(lane >= HALF, jnp.logical_not(odd))
    mine6 = jnp.logical_or(lane < HALF, odd)
    tile0 = jnp.where(mine0, full_ref[:, :TILE], LOW)
    tile6 = jnp.where(mine6, full_ref[:, last:], LOW)
    mid = full_ref[:, TILE:last]
    biggest = lambda x: jnp.max(x, axis=1, keepdims=True)
    top = jnp.maximum(biggest(mid), biggest(jnp.maximum(tile0, tile6)))
    mid = jnp.exp(mid - top)
    tile0 = jnp.where(mine0, jnp.exp(tile0 - top), 0.0)
    tile6 = jnp.where(mine6, jnp.exp(tile6 - top), 0.0)
    total = jnp.sum(mid, axis=1, keepdims=True) + jnp.sum(tile0 + tile6, axis=1, keepdims=True)
    stats = stat_lanes(top, total, rows)
    out_ref[:, :TILE] = jnp.where(mine0, tile0, stats).astype(BF16)
    out_ref[:, TILE:last] = mid.astype(BF16)
    out_ref[:, last:] = jnp.where(mine6, tile6, stats).astype(BF16)


def softmax_of(full, embed_other):
    return pl.pallas_call(
        softmax_kernel,
        out_shape=jax.ShapeDtypeStruct(full.shape, BF16),
        in_specs=[VMEM, HBM],
        out_specs=VMEM,
        cost_estimate=cost(1 << 20, 1 << 20),
        compiler_params=limit,
        name="softmax",
    )(full, stay(embed_other))


def mix_kernel(order, ahead, n_in, *refs):
    first, last = order == (0,), 4 in order
    blocks, refs = refs[:n_in], refs[n_in:]
    if last:
        (ready_ref, old_ref, old_stat_ref), (out_ref, w_ref, ship_ref) = refs[:3], refs[3:]
    else:
        tables, refs = refs[:2], refs[2:]
        if not first:
            old_ref, old_stat_ref, refs = refs[0], refs[1], refs[2:]
        out_ref, stat_ref, zero_ref, zero2_ref, refs = *refs[:4], refs[4:]
        if ahead:
            ahead_ref, refs = refs[0], refs[1:]
        w_ref, ready_ref, sem = refs
    n, rows, width = w_ref.shape
    feats = ready_ref.shape[2]
    nt = lambda a, b: lax.dot_general(a, b, (((1,), (1,)), ((), ())), preferred_element_type=F32)
    lane = iota(rows)
    tail = width - TILE

    def copies(d, to, slot):
        return [
            pltpu.make_async_copy(tables[k].at[:, window(d, width)], to.at[k], sem.at[slot, k])
            for k in range(2)
        ]

    now, later = [], []
    if not last:
        now = [copies(d, ready_ref.at[slot], slot) for slot, d in enumerate(order)]
        later = [c for k, d in enumerate(ahead) for c in copies(d, ahead_ref.at[k], n + k)]
    for copy in [c for pair in now for c in pair] + later:
        copy.start()
    sums, tops, totals = [], [], []
    for slot, d in enumerate(order):
        w_ref[slot] = blocks[slot][...]
        odd = (chunk_of(d) & 1) == 1
        tile0, tile6 = w_ref[slot, :, :TILE].astype(F32), w_ref[slot, :, tail:].astype(F32)
        top, total = read_lanes(jnp.where(odd, tile0, tile6), lane - jnp.where(odd, 0, HALF))
        tops.append(top)
        totals.append(total)
        low = jnp.logical_and(odd, lane < HALF)
        high = jnp.logical_and(jnp.logical_not(odd), lane >= HALF)
        w_ref[slot, :, :TILE] = jnp.where(low, 0.0, tile0).astype(BF16)
        w_ref[slot, :, tail:] = jnp.where(high, 0.0, tile6).astype(BF16)
    for slot in range(n):
        for copy in now[slot] if now else []:
            copy.wait()
        sums.append([nt(w_ref[slot], ready_ref[slot, k]) for k in range(2)])
    if not first:
        tops.append(old_stat_ref[:, 0:1])
        totals.append(old_stat_ref[:, 1:2])
        sums.append((old_ref[0, :, :feats], old_ref[1, :, :feats]))
    top = tops[0]
    for t in tops[1:]:
        top = jnp.maximum(top, t)
    factors = [jnp.exp(t - top) for t in tops]
    total = sum(t * f for t, f in zip(totals, factors))
    mine, others = [sum(s[k] * f for s, f in zip(sums, factors)) for k in range(2)]
    if not last:
        out_ref[0, :, :feats] = mine
        out_ref[1, :, :feats] = others
        stat_ref[...] = jnp.where(lane == 0, top, total)
        zero_ref[...] = jnp.zeros_like(zero_ref)
        zero2_ref[...] = jnp.zeros_like(zero2_ref)
        for copy in later:
            copy.wait()
        return
    stats = stat_lanes(top, total, rows)
    z, core = here()
    cut = feats // TILE * TILE
    for k, value in enumerate((mine, others)):
        ship_ref[k, :, :cut] = value[:, :cut].astype(BF16)
        ship_ref[k, :, cut:] = jnp.concatenate(
            [value[:, cut:], stats[:, : TILE - (feats - cut)]], 1
        ).astype(BF16)
    for dz in range(8):
        at = pl.ds(pl.multiple_of(((z + dz) & 7) * 16, 16), 16)
        spots = [((z >> 1) + rel // 4 & 3) * 4 + (2 * z + rel % 4 & 3) for rel in PLACE[2 * dz : 2 * dz + 2]]
        out_ref[jnp.where(core == 0, spots[0], spots[1])] = ship_ref[0, at, :]
        out_ref[jnp.where(core == 0, spots[1], spots[0])] = ship_ref[1, at, :]


def mix_of(order, blocks, tables, ready, old, ahead=()):
    n, last = len(order), 4 in order
    rows, width = blocks[0].shape
    feats = tables[0].shape[0]
    wide = pl.cdiv(feats, TILE) * TILE
    scratch = [pltpu.VMEM((n, rows, width), BF16)]
    if last:
        tables = []
        out_shape = [jax.ShapeDtypeStruct((rows // 8, 16, wide), BF16)]
        scratch.append(pltpu.VMEM((2, rows, wide), BF16))
    else:
        out_shape = [
            jax.ShapeDtypeStruct((2, rows, wide), F32),
            jax.ShapeDtypeStruct((rows, TILE), F32),
            jax.ShapeDtypeStruct((1, width), BF16),
            jax.ShapeDtypeStruct((1, width), BF16),
        ]
        if ahead:
            out_shape.append(jax.ShapeDtypeStruct((len(ahead), 2, feats, width), BF16))
        scratch.append(pltpu.VMEM((n, 2, feats, width), BF16))
        scratch.append(pltpu.SemaphoreType.DMA((n + len(ahead), 2)))
    specs = [VMEM] * len(blocks) + [HBM] * len(tables)
    return pl.pallas_call(
        lambda *refs: mix_kernel(order, ahead, len(blocks), *refs),
        out_shape=out_shape,
        in_specs=specs + [VMEM] * len(ready + old),
        out_specs=[VMEM] * len(out_shape),
        scratch_shapes=scratch,
        cost_estimate=cost(4 * n * rows * feats * width, 4 * n * feats * width),
        compiler_params=limit,
        name=f"mix{n}{'l' if last else ''}",
    )(*blocks, *[stay(t) for t in tables], *ready, *old)


def combine_kernel(got_ref, out_ref):
    parts, rows, wide = got_ref.shape
    feats = out_ref.shape[1]
    lane = iota(rows) - (feats - (wide - TILE))
    stats = [read_lanes(got_ref[v, :, wide - TILE :].astype(F32), lane) for v in range(parts)]
    top = stats[0][0]
    for t, _ in stats[1:]:
        top = jnp.maximum(top, t)
    factors = [jnp.exp(t - top) for t, _ in stats]
    total = sum(t * f for (_, t), f in zip(stats, factors))
    mixture = sum(got_ref[v].astype(F32) * f for v, f in enumerate(factors))
    out_ref[...] = (mixture / total)[:, :feats].astype(BF16)


def combine(got, feats):
    return pl.pallas_call(
        combine_kernel,
        out_shape=jax.ShapeDtypeStruct((got.shape[1], feats), BF16),
        in_specs=[VMEM],
        out_specs=VMEM,
        cost_estimate=cost(1 << 18, 1 << 18),
        compiler_params=limit,
        name="combine",
    )(got)


def on_device(hidden, head_table, embed_table):
    me = lax.axis_index("dp")
    z, core = me // 2, me % 2
    size = lax.axis_size("dp")
    chips = size // 2
    rows_dev = hidden.shape[0]
    feats, vocab = head_table.shape
    rows = chips * rows_dev
    pair = vocab // TILE // (chips // 2)
    width = (pair // 2 + 1) * TILE

    swap = lambda x: lax.ppermute(x, "dp", [(i, i ^ 1) for i in range(size)])
    side = [2 - 4 * (i % 2) for i in range(size)]
    up = lambda x: lax.ppermute(x, "dp", [(i, (i + side[i]) % size) for i in range(size)])
    down = lambda x: lax.ppermute(x, "dp", [(i, (i - side[i]) % size) for i in range(size)])
    up2 = lambda x: lax.ppermute(x, "dp", [(i, (i + 2 * side[i]) % size) for i in range(size)])
    enc = lambda x: (x * SCALE).astype(WIRE)
    dec = lambda x: x.astype(F32) * (1.0 / SCALE)

    groups = [[c + 2 * k for k in range(chips)] for c in range(2)]
    slices = lax.all_to_all(deal(hidden, chips), "dp", 0, 0, axis_index_groups=groups)
    slices = slices.reshape(rows, 2 * feats)
    head_other = swap(head_table)
    embed_own = embed_table.T
    embed_other = swap(embed_own)
    first, second = slices[:, :feats], slices[:, feats:]
    own = jnp.where(core == 0, first, second)
    others = jnp.where(core == 0, second, first)

    logits = lambda order: logits_of(order, own, others, [head_table, head_other], width)
    far, p3, m3 = logits((4, 3, 5))
    a4, a, b = up2(enc(far)), up(enc(p3)), down(enc(m3))
    p2, m2, p1, m1, p0 = logits((2, 6, 1, 7, 0))
    a = up(enc(p2 + dec(a) + dec(a4)))
    b = down(enc(m2 + dec(b)))
    a = up(enc(p1 + dec(a)))
    b = down(enc(m1 + dec(b)))
    full = p0 + dec(a) + dec(b)

    block = softmax_of(full, embed_other)
    tables = [embed_own, embed_other]
    mix = lambda order, blocks, old, **kw: mix_of(order, blocks, tables, [], old, **kw)
    a1 = up(block)
    *state, za, zb = mix((0,), [block], [])
    b1 = down(block + zb)
    a2 = up(a1 + za)
    *state, za, zb = mix((7,), [a1], state)
    b2 = down(b1 + zb)
    a2_sent = a2 + za
    a4, a3 = up2(a2_sent), up(a2_sent)
    b3 = down(b2)
    *state, _, _ = mix((1, 6), [b1, a2], state)
    *state, _, _, ready = mix((2, 5), [b2, a3], state, ahead=(3, 4))
    (blocks,) = mix_of((3, 4), [b3, a4], tables, [ready], state)

    result = combine(lax.all_to_all(blocks, "vocab", 0, 0), feats)
    flip = []
    for k in range(chips):
        for c in range(2):
            for r in range(chips):
                for f in range(2):
                    here = (2 * k + c) * size + place(k, r, f)
                    there = (2 * r + c) * size + 2 * k + f
                    flip.append((here, there))
    return lax.ppermute(result, ("dp", "vocab"), flip)


def solution(mesh):
    in_specs = (P("dp", None), P("dp", "vocab"), P("vocab", "dp"))
    out_specs = P("dp", "vocab")
    return jax.shard_map(
        on_device, mesh=mesh, in_specs=in_specs, out_specs=out_specs, check_vma=False
    )
```

time: 313 us -> 113 us (0.36)
  waiting for transfers between devices: 183 us -> 43.5 us
  blocking collectives: 83.6 us -> 13.2 us
  starting transfers between devices: 5.47 us -> 31.9 us
  Pallas kernels: 0 us -> 21.1 us
  matrix products: 13.9 us -> 0 us
  between operations: 13.4 us -> 0.22 us
  other arithmetic: 8.03 us -> 0.96 us
  local copies, waits for them, and re-layouts: 5 us -> 0.61 us
    psum x1 -> x0, waiting for transfers between devices: 128 us -> none  [on_device(): lax.psum(jnp.dot(slices, head_table, preferred_element_type=jnp.float32),...]
    unnamed x3 -> x0, waiting for transfers between devices: 43.7 us -> none
    pmax x1 -> x0, blocking collectives: 33.3 us -> none  [row_stats(): row_top = lax.pmax(local_top, 'vocab')]
    ppermute x0 -> x17, waiting for transfers between devices: none -> 32.2 us  [the longest x6 21.3 us: on_device(): lax.ppermute(x, 'dp', [(i, (i + side[i]) % size) for i in range(size)])]
    psum x1 -> x0, blocking collectives: 30.8 us -> none  [row_stats(): row_total = lax.psum(jnp.sum(scaled, axis=1, keepdims=True), 'vocab')]
    ppermute x0 -> x17, starting transfers between devices: none -> 23.4 us  [the longest x6 14 us: on_device(): lax.ppermute(x, 'dp', [(i, (i - side[i]) % size) for i in range(size)])]
    pallas_call x0 -> x10, Pallas kernels: none -> 21.1 us  [the longest x5 12.1 us: mix_of(): pl.pallas_call(lambda *refs: mix_kernel(order, ahead, len(blocks), *refs)...]
    dot_general x2 -> x0, matrix products: 13.9 us -> none  [the longest x1 7.5 us: on_device(): jnp.dot(slices, head_table, preferred_element_type=jnp.float32)]
  transfers between devices with their start and end apart: 3 -> 18, of which waited for: 3 -> 10; matrix products, arithmetic and copies ran while one was open for 1% -> 1% of each run, Pallas kernels for 0% -> 17%
where the time goes in v3:
time: 113 us; the launch traced here: 111 us
  waiting for transfers between devices  43.5 us (38%)
  starting transfers between devices  31.9 us (28%)
  Pallas kernels  21.1 us (19%)
  blocking collectives  13.2 us (12%)
    ppermute x6, waiting for transfers between devices, on_device(): lax.ppermute(x, 'dp', [(i, (i + side[i]) % size) for i in range(size)])  21.3 us
    ppermute x6, starting transfers between devices, on_device(): lax.ppermute(x, 'dp', [(i, (i - side[i]) % size) for i in range(size)])  14 us
    all_to_all x1, blocking collectives, on_device(): result = combine(lax.all_to_all(blocks, 'vocab', 0, 0), feats)  13.2 us
    pallas_call x5, Pallas kernels, mix_of(): pl.pallas_call(lambda *refs: mix_kernel(order, ahead, len(blocks), *refs)...  12.1 us
    all_to_all x1, waiting for transfers between devices, on_device(): lax.all_to_all(deal(hidden, chips), 'dp', 0, 0, axis_index_groups=groups)  11.3 us
    all_to_all x1, starting transfers between devices, on_device(): lax.all_to_all(deal(hidden, chips), 'dp', 0, 0, axis_index_groups=groups)  8.48 us
    pallas_call x2, Pallas kernels, logits_of(): pl.pallas_call(lambda *refs: logits_kernel(order, *refs), out_shape=[jax....  6.89 us
    ppermute x6, waiting for transfers between devices, on_device(): lax.ppermute(x, 'dp', [(i, (i - side[i]) % size) for i in range(size)])  5.74 us
  transfers between devices with their start and end apart: 18, of which 10 were waited for; matrix products, arithmetic and copies ran while one was open for 1% of the time, Pallas kernels for 17%

profile of v3, /device:TPU:16, one launch (start us, length us, event | category | flops | bytes accessed | tf_op | source)
XLA Modules:
  0.0 111.4 jit_solution(14500130875479221681)
XLA Ops:
  0.0 0.5 collective-permute-start.8
  0.5 1.6 %deal.1 = bf16[8,16,896]{2,1,0:T(8,128)(2,1)} custom-call(bf16[16,7168]{1,0:T(8,128)(2,1)} %hidden_ref.1), custom_call_target="tpu_custom_call" | custom-call | bytes 524288 | tf_op jit(solution)/shard_map/deal/pallas_call | solution.py:84
  2.1 8.5 %all-to-all-start = ((bf16[8,16,896]{2,1,0:T(8,128)(2,1)}), bf16[8,16,896]{2,1,0:T(8,128)(2,1)S(1)}, u32[]{:S(2)}, u32[]{:S(2)}) async-start(bf16[8,16,896]{2,1,0:T(8,128)(2,1)} %deal.1), calls=%async_computation | async-start | bytes 458752 | tf_op jit(solution)/shard_map/all_to_all | solution.py:329
  10.6 11.3 %all-to-all-done = bf16[8,16,896]{2,1,0:T(8,128)(2,1)S(1)} async-done(((bf16[8,16,896]{2,1,0:T(8,128)(2,1)}), bf16[8,16,896]{2,1,0:T(8,128)(2,1)S(1)}, u32[]{:S(2)}, u32[]{:S(2)}) %all-to-all-start) | async-done | bytes 229408 | tf_op jit(solution)/shard_map/all_to_all | solution.py:329
  22.0 0.1 broadcast_select_fusion
  22.1 2.9 %logits3.1 = (f32[128,896]{1,0:T(8,128)S(1)}, f32[128,896]{1,0:T(8,128)S(1)}, f32[128,896]{1,0:T(8,128)S(1)}) custom-call(bf16[128,448]{1,0:T(8,128)(2,1)S(1)} %get-tuple-element.48.refs_0_, bf16[128,448]{1,0:T(8,128)(2,1)S(1)} %get-tuple-element.47.refs_1_, bf16[448,6656]{1,0:T(8,128)(2,1)} %refs_2_.3, bf16[448,6656]{1,0:T(8,128)(2,1)} %collective-permute-done.refs_3_), custom_call_target="tpu_custom_call" | custom-call | flops 616562688 | bytes 4816896 | tf_op jit(solution)/shard_map/logits3/pallas_call | solution.py:119
  25.1 0.6 collective-permute-start.1
  25.7 0.6 collective-permute-start.2
  26.4 2.3 %collective-permute-start.5 = (f16[128,896]{1,0:T(8,128)(2,1)S(1)}, f16[128,896]{1,0:T(8,128)(2,1)S(1)}, u32[]{:S(2)}, u32[]{:S(2)}) collective-permute-start(f16[128,896]{1,0:T(8,128)(2,1)S(1)} %multiply_convert_fusion.2), channel_id=1, source_target_pairs={{0,224},{16,48},{32,0},{48,80},{64,32},{80,112},{96,64},{112,144},... | collective-permute-start | bytes 688136 | tf_op jit(solution)/shard_map/ppermute | solution.py:323
  28.7 4.0 %logits5.1 = (f32[128,896]{1,0:T(8,128)S(1)}, f32[128,896]{1,0:T(8,128)S(1)}, f32[128,896]{1,0:T(8,128)S(1)}, f32[128,896]{1,0:T(8,128)S(1)}, f32[128,896]{1,0:T(8,128)S(1)}) custom-call(bf16[128,448]{1,0:T(8,128)(2,1)S(1)} %get-tuple-element.48.refs_0_, bf16[128,448]{1,0:T(8,128)(2,1)S(1)} %get-tuple-element.47.refs_1_, bf16[448,6656]{1,0:T(8,128)(2,1)} %refs_2_.3, ...), custom_call_target="tpu_custom_call" | custom-call | flops 1027604480 | bytes 8028160 | tf_op jit(solution)/shard_map/logits5/pallas_call | solution.py:119
  32.7 3.4 %collective-permute-done.1 = f16[128,896]{1,0:T(8,128)(2,1)S(1)} collective-permute-done((f16[128,896]{1,0:T(8,128)(2,1)S(1)}, f16[128,896]{1,0:T(8,128)(2,1)S(1)}, u32[]{:S(2)}, u32[]{:S(2)}) %collective-permute-start.1) | collective-permute-done | bytes 229408 | tf_op jit(solution)/shard_map/ppermute | solution.py:322
  36.1 0.0 collective-permute-done.2
  36.1 0.1 multiply_convert_fusion.4
  36.3 4.0 %collective-permute-start.3 = (f16[128,896]{1,0:T(8,128)(2,1)S(1)}, f16[128,896]{1,0:T(8,128)(2,1)S(1)}, u32[]{:S(2)}, u32[]{:S(2)}) collective-permute-start(f16[128,896]{1,0:T(8,128)(2,1)S(1)} %multiply_convert_fusion.4), channel_id=1, source_target_pairs={{0,32},{16,240},{32,64},{48,16},{64,96},{80,48},{96,128},{112,80},... | collective-permute-start | bytes 688136 | tf_op jit(solution)/shard_map/ppermute | solution.py:322
  40.3 0.1 multiply_convert_fusion.1
  40.3 0.1 collective-permute-start.6
  40.4 5.4 %collective-permute-done.3 = f16[128,896]{1,0:T(8,128)(2,1)S(1)} collective-permute-done((f16[128,896]{1,0:T(8,128)(2,1)S(1)}, f16[128,896]{1,0:T(8,128)(2,1)S(1)}, u32[]{:S(2)}, u32[]{:S(2)}) %collective-permute-start.3) | collective-permute-done | bytes 229408 | tf_op jit(solution)/shard_map/ppermute | solution.py:322
  45.8 0.1 multiply_convert_fusion.3
  45.9 0.6 collective-permute-start.4
  46.5 1.6 %collective-permute-done.6 = f16[128,896]{1,0:T(8,128)(2,1)S(1)} collective-permute-done((f16[128,896]{1,0:T(8,128)(2,1)S(1)}, f16[128,896]{1,0:T(8,128)(2,1)S(1)}, u32[]{:S(2)}, u32[]{:S(2)}) %collective-permute-start.6) | collective-permute-done | bytes 229408 | tf_op jit(solution)/shard_map/ppermute | solution.py:323
  48.0 0.1 multiply_convert_fusion
  48.1 1.3 %collective-permute-start.7 = (f16[128,896]{1,0:T(8,128)(2,1)S(1)}, f16[128,896]{1,0:T(8,128)(2,1)S(1)}, u32[]{:S(2)}, u32[]{:S(2)}) collective-permute-start(f16[128,896]{1,0:T(8,128)(2,1)S(1)} %multiply_convert_fusion), channel_id=1, source_target_pairs={{0,224},{16,48},{32,0},{48,80},{64,32},{80,112},{96,64},{112,144},... | collective-permute-start | bytes 688136 | tf_op jit(solution)/shard_map/ppermute | solution.py:323
  49.4 5.4 %collective-permute-done.4 = f16[128,896]{1,0:T(8,128)(2,1)S(1)} collective-permute-done((f16[128,896]{1,0:T(8,128)(2,1)S(1)}, f16[128,896]{1,0:T(8,128)(2,1)S(1)}, u32[]{:S(2)}, u32[]{:S(2)}) %collective-permute-start.4) | collective-permute-done | bytes 229408 | tf_op jit(solution)/shard_map/ppermute | solution.py:322
  54.8 0.0 collective-permute-done.7
  54.8 0.1 multiply_add_fusion.full_ref
  54.9 0.0 collective-permute-done.8.unused_ref.refs_2_.refs_3_
  54.9 0.3 softmax.1.refs_0_
  55.2 0.2 collective-permute-start.10
  55.4 2.1 %mix1.2 = (f32[2,128,512]{2,1,0:T(8,128)S(1)}, f32[128,128]{1,0:T(8,128)S(1)}, bf16[1,896]{1,0:T(2,128)(2,1)S(1)}, bf16[1,896]{1,0:T(2,128)(2,1)S(1)}) custom-call(bf16[128,896]{1,0:T(8,128)(2,1)S(1)} %softmax.1.refs_0_, bf16[448,6656]{1,0:T(8,128)(2,1)} %bitcast.3, bf16[448,6656]{1,0:T(8,128)(2,1)} %collective-permute-done.8.unused_ref.refs_2_.refs_3_), custom_call_target="tpu_custom_call" | custom-call | flops 205520896 | bytes 1605632 | tf_op jit(solution)/shard_map/mix1/pallas_call | solution.py:271
  57.6 3.4 %collective-permute-start.9 = (bf16[128,896]{1,0:T(8,128)(2,1)S(1)}, bf16[128,896]{1,0:T(8,128)(2,1)S(1)}, u32[]{:S(2)}, u32[]{:S(2)}) collective-permute-start(bf16[128,896]{1,0:T(8,128)(2,1)S(1)} %broadcast_add_fusion.3), channel_id=1, source_target_pairs={{0,224},{16,48},{32,0},{48,80},{64,32},{80,112},{96,64},{112,144},... | collective-permute-start | bytes 688136 | tf_op jit(solution)/shard_map/ppermute | solution.py:323
  60.9 3.3 %collective-permute-done.10.refs_0_ = bf16[128,896]{1,0:T(8,128)(2,1)S(1)} collective-permute-done((bf16[128,896]{1,0:T(8,128)(2,1)S(1)}, bf16[128,896]{1,0:T(8,128)(2,1)S(1)}, u32[]{:S(2)}, u32[]{:S(2)}) %collective-permute-start.10) | collective-permute-done | bytes 229408 | tf_op jit(solution)/shard_map/ppermute | solution.py:322
  64.3 0.1 collective-permute-start.13
  64.4 2.1 %mix1.3 = (f32[2,128,512]{2,1,0:T(8,128)S(1)}, f32[128,128]{1,0:T(8,128)S(1)}, bf16[1,896]{1,0:T(2,128)(2,1)S(1)}, bf16[1,896]{1,0:T(2,128)(2,1)S(1)}) custom-call(bf16[128,896]{1,0:T(8,128)(2,1)S(1)} %collective-permute-done.10.refs_0_, bf16[448,6656]{1,0:T(8,128)(2,1)} %bitcast.4, bf16[448,6656]{1,0:T(8,128)(2,1)} %collective-permute-done.8.unused_ref.refs_2_.refs_3_, ...), custom_call_target="tpu_custom_call" | custom-call | flops 205520896 | bytes 1605632 | tf_op jit(solution)/shard_map/mix1/pallas_call | solution.py:271
  66.5 0.5 collective-permute-done.9.refs_0_
  67.1 2.8 %collective-permute-start.11 = (bf16[128,896]{1,0:T(8,128)(2,1)S(1)}, bf16[128,896]{1,0:T(8,128)(2,1)S(1)}, u32[]{:S(2)}, u32[]{:S(2)}) collective-permute-start(bf16[128,896]{1,0:T(8,128)(2,1)S(1)} %broadcast_add_fusion.2), channel_id=1, source_target_pairs={{0,224},{16,48},{32,0},{48,80},{64,32},{80,112},{96,64},{112,144},... | collective-permute-start | bytes 688136 | tf_op jit(solution)/shard_map/ppermute | solution.py:323
  69.9 3.8 %collective-permute-done.13.refs_1_ = bf16[128,896]{1,0:T(8,128)(2,1)S(1)} collective-permute-done((bf16[128,896]{1,0:T(8,128)(2,1)S(1)}, bf16[128,896]{1,0:T(8,128)(2,1)S(1)}, u32[]{:S(2)}, u32[]{:S(2)}) %collective-permute-start.13) | collective-permute-done | bytes 229408 | tf_op jit(solution)/shard_map/ppermute | solution.py:322
  73.6 0.1 collective-permute-start.15
  73.7 0.1 collective-permute-start.14
  73.8 3.7 %collective-permute-done.11.refs_0_ = bf16[128,896]{1,0:T(8,128)(2,1)S(1)} collective-permute-done((bf16[128,896]{1,0:T(8,128)(2,1)S(1)}, bf16[128,896]{1,0:T(8,128)(2,1)S(1)}, u32[]{:S(2)}, u32[]{:S(2)}) %collective-permute-start.11) | collective-permute-done | bytes 229408 | tf_op jit(solution)/shard_map/ppermute | solution.py:323
  77.5 4.2 %collective-permute-start.12 = (bf16[128,896]{1,0:T(8,128)(2,1)S(1)}, bf16[128,896]{1,0:T(8,128)(2,1)S(1)}, u32[]{:S(2)}, u32[]{:S(2)}) collective-permute-start(bf16[128,896]{1,0:T(8,128)(2,1)S(1)} %collective-permute-done.11.refs_0_), channel_id=1, source_target_pairs={{0,224},{16,48},{32,0},{48,80},{64,32},{80,112},{96,64},{112,144},... | collective-permute-start | bytes 688136 | tf_op jit(solution)/shard_map/ppermute | solution.py:323
  81.7 3.2 %mix2.2 = (f32[2,128,512]{2,1,0:T(8,128)S(1)}, f32[128,128]{1,0:T(8,128)S(1)}, bf16[1,896]{1,0:T(2,128)(2,1)}, bf16[1,896]{1,0:T(2,128)(2,1)}) custom-call(bf16[128,896]{1,0:T(8,128)(2,1)S(1)} %collective-permute-done.9.refs_0_, bf16[128,896]{1,0:T(8,128)(2,1)S(1)} %collective-permute-done.13.refs_1_, bf16[448,6656]{1,0:T(8,128)(2,1)} %bitcast.5, ...), custom_call_target="tpu_custom_call" | custom-call | flops 411041792 | bytes 3211264 | tf_op jit(solution)/shard_map/mix2/pallas_call | solution.py:271
  84.9 3.6 %mix2.3 = (f32[2,128,512]{2,1,0:T(8,128)S(1)}, f32[128,128]{1,0:T(8,128)S(1)}, bf16[1,896]{1,0:T(2,128)(2,1)}, bf16[1,896]{1,0:T(2,128)(2,1)}, bf16[2,2,448,896]{3,2,1,0:T(8,128)(2,1)S(1)}) custom-call(bf16[128,896]{1,0:T(8,128)(2,1)S(1)} %collective-permute-done.11.refs_0_, bf16[128,896]{1,0:T(8,128)(2,1)S(1)} %collective-permute-done.15.refs_1_, ...), custom_call_target="tpu_custom_call" | custom-call | flops 411041792 | bytes 3211264 | tf_op jit(solution)/shard_map/mix2/pallas_call | solution.py:271
  88.5 1.2 %mix2l.1 = bf16[16,16,512]{2,1,0:T(8,128)(2,1)S(1)} custom-call(bf16[128,896]{1,0:T(8,128)(2,1)S(1)} %collective-permute-done.12.refs_0_, bf16[128,896]{1,0:T(8,128)(2,1)S(1)} %collective-permute-done.14.refs_1_, bf16[2,2,448,896]{3,2,1,0:T(8,128)(2,1)S(1)} %get-tuple-element.44.refs_2_, f32[2,128,512]{2,1,0:T(8,128)S(1)} %get-tuple-element.45.refs_3_, ...), custom_call_target="tpu_custom_call" | custom-call | flops 411041792 | bytes 3211264 | tf_op jit(solution)/shard_map/mix2l/pallas_call | solution.py:271
  89.7 13.2 %all_to_all.10.got_ref = bf16[16,16,512]{2,1,0:T(8,128)(2,1)S(1)} all-to-all(bf16[16,16,512]{2,1,0:T(8,128)(2,1)S(1)} %mix2l.1), channel_id=1, replica_groups=mesh['dp'=16,'vocab'=16] {'vocab'}, dimensions={0} | all-to-all | bytes 524288 | tf_op jit(solution)/shard_map/all_to_all | solution.py:364
  102.9 0.2 combine.1
  103.1 2.6 %collective-permute-start.16 = (bf16[16,448]{1,0:T(8,128)(2,1)S(1)}, bf16[16,448]{1,0:T(8,128)(2,1)S(1)}, u32[]{:S(2)}, u32[]{:S(2)}) collective-permute-start(bf16[16,448]{1,0:T(8,128)(2,1)S(1)} %combine.1), channel_id=1, source_target_pairs={{7,0},{2,1},{11,32},{6,33},{3,64},{14,65},{12,96},{13,97},{0,128},... | collective-permute-start | bytes 43016 | tf_op jit(solution)/shard_map/ppermute | solution.py:373
  105.7 5.1 %collective-permute-done.16 = bf16[16,448]{1,0:T(8,128)(2,1)S(1)} collective-permute-done((bf16[16,448]{1,0:T(8,128)(2,1)S(1)}, bf16[16,448]{1,0:T(8,128)(2,1)S(1)}, u32[]{:S(2)}, u32[]{:S(2)}) %collective-permute-start.16) | collective-permute-done | bytes 14368 | tf_op jit(solution)/shard_map/ppermute | solution.py:373
  110.8 0.6 copy.5
  (17 shorter events, 0.3 us)
Async XLA Ops:
  0.0 22.1 %collective-permute-start = (bf16[448,6656]{1,0:T(8,128)(2,1)}, bf16[448,6656]{1,0:T(8,128)(2,1)}, u32[]{:S(2)}, u32[]{:S(2)}) collective-permute-start(bf16[448,6656]{1,0:T(8,128)(2,1)} %refs_2_.3), channel_id=1, source_target_pairs={{0,16},{16,0},{32,48},{48,32},{64,80},{80,64},{96,112},{112,96},{1... | collective-permute-start | bytes 17891336 | tf_op jit(solution)/shard_map/ppermute | solution.py:320
  0.0 54.9 %collective-permute-start.8 = (bf16[448,6656]{1,0:T(8,128)(2,1)}, bf16[448,6656]{1,0:T(8,128)(2,1)}, u32[]{:S(2)}, u32[]{:S(2)}) collective-permute-start(bf16[448,6656]{1,0:T(8,128)(2,1)} %bitcast.2), channel_id=1, source_target_pairs={{0,16},{16,0},{32,48},{48,32},{64,80},{80,64},{96,112},{112,96},{1... | collective-permute-start | bytes 17891336 | tf_op jit(solution)/shard_map/ppermute | solution.py:320
  2.1 19.8 %all-to-all-start = ((bf16[8,16,896]{2,1,0:T(8,128)(2,1)}), bf16[8,16,896]{2,1,0:T(8,128)(2,1)S(1)}, u32[]{:S(2)}, u32[]{:S(2)}) async-start(bf16[8,16,896]{2,1,0:T(8,128)(2,1)} %deal.1), calls=%async_computation | async-start | bytes 458752 | tf_op jit(solution)/shard_map/all_to_all | solution.py:329
  25.1 11.1 %collective-permute-start.1 = (f16[128,896]{1,0:T(8,128)(2,1)S(1)}, f16[128,896]{1,0:T(8,128)(2,1)S(1)}, u32[]{:S(2)}, u32[]{:S(2)}) collective-permute-start(f16[128,896]{1,0:T(8,128)(2,1)S(1)} %multiply_convert_fusion.6), channel_id=1, source_target_pairs={{0,32},{16,240},{32,64},{48,16},{64,96},{80,48},{96,128},{112,80},... | collective-permute-start | bytes 688136 | tf_op jit(solution)/shard_map/ppermute | solution.py:322
  25.7 10.4 %collective-permute-start.2 = (f16[128,896]{1,0:T(8,128)(2,1)S(1)}, f16[128,896]{1,0:T(8,128)(2,1)S(1)}, u32[]{:S(2)}, u32[]{:S(2)}) collective-permute-start(f16[128,896]{1,0:T(8,128)(2,1)S(1)} %multiply_convert_fusion.5), channel_id=1, source_target_pairs={{0,64},{16,208},{32,96},{48,240},{64,128},{80,16},{96,160},{112,48... | collective-permute-start | bytes 688136 | tf_op jit(solution)/shard_map/ppermute | solution.py:324
  26.4 13.8 %collective-permute-start.5 = (f16[128,896]{1,0:T(8,128)(2,1)S(1)}, f16[128,896]{1,0:T(8,128)(2,1)S(1)}, u32[]{:S(2)}, u32[]{:S(2)}) collective-permute-start(f16[128,896]{1,0:T(8,128)(2,1)S(1)} %multiply_convert_fusion.2), channel_id=1, source_target_pairs={{0,224},{16,48},{32,0},{48,80},{64,32},{80,112},{96,64},{112,144},... | collective-permute-start | bytes 688136 | tf_op jit(solution)/shard_map/ppermute | solution.py:323
  36.3 9.5 %collective-permute-start.3 = (f16[128,896]{1,0:T(8,128)(2,1)S(1)}, f16[128,896]{1,0:T(8,128)(2,1)S(1)}, u32[]{:S(2)}, u32[]{:S(2)}) collective-permute-start(f16[128,896]{1,0:T(8,128)(2,1)S(1)} %multiply_convert_fusion.4), channel_id=1, source_target_pairs={{0,32},{16,240},{32,64},{48,16},{64,96},{80,48},{96,128},{112,80},... | collective-permute-start | bytes 688136 | tf_op jit(solution)/shard_map/ppermute | solution.py:322
  40.3 7.7 %collective-permute-start.6 = (f16[128,896]{1,0:T(8,128)(2,1)S(1)}, f16[128,896]{1,0:T(8,128)(2,1)S(1)}, u32[]{:S(2)}, u32[]{:S(2)}) collective-permute-start(f16[128,896]{1,0:T(8,128)(2,1)S(1)} %multiply_convert_fusion.1), channel_id=1, source_target_pairs={{0,224},{16,48},{32,0},{48,80},{64,32},{80,112},{96,64},{112,144},... | collective-permute-start | bytes 688136 | tf_op jit(solution)/shard_map/ppermute | solution.py:323
  45.9 8.9 %collective-permute-start.4 = (f16[128,896]{1,0:T(8,128)(2,1)S(1)}, f16[128,896]{1,0:T(8,128)(2,1)S(1)}, u32[]{:S(2)}, u32[]{:S(2)}) collective-permute-start(f16[128,896]{1,0:T(8,128)(2,1)S(1)} %multiply_convert_fusion.3), channel_id=1, source_target_pairs={{0,32},{16,240},{32,64},{48,16},{64,96},{80,48},{96,128},{112,80},... | collective-permute-start | bytes 688136 | tf_op jit(solution)/shard_map/ppermute | solution.py:322
  48.1 6.7 %collective-permute-start.7 = (f16[128,896]{1,0:T(8,128)(2,1)S(1)}, f16[128,896]{1,0:T(8,128)(2,1)S(1)}, u32[]{:S(2)}, u32[]{:S(2)}) collective-permute-start(f16[128,896]{1,0:T(8,128)(2,1)S(1)} %multiply_convert_fusion), channel_id=1, source_target_pairs={{0,224},{16,48},{32,0},{48,80},{64,32},{80,112},{96,64},{112,144},... | collective-permute-start | bytes 688136 | tf_op jit(solution)/shard_map/ppermute | solution.py:323
  55.2 9.1 %collective-permute-start.10 = (bf16[128,896]{1,0:T(8,128)(2,1)S(1)}, bf16[128,896]{1,0:T(8,128)(2,1)S(1)}, u32[]{:S(2)}, u32[]{:S(2)}) collective-permute-start(bf16[128,896]{1,0:T(8,128)(2,1)S(1)} %softmax.1.refs_0_), channel_id=1, source_target_pairs={{0,32},{16,240},{32,64},{48,16},{64,96},{80,48},{96,128},{112,80},... | collective-permute-start | bytes 688136 | tf_op jit(solution)/shard_map/ppermute | solution.py:322
  57.6 9.5 %collective-permute-start.9 = (bf16[128,896]{1,0:T(8,128)(2,1)S(1)}, bf16[128,896]{1,0:T(8,128)(2,1)S(1)}, u32[]{:S(2)}, u32[]{:S(2)}) collective-permute-start(bf16[128,896]{1,0:T(8,128)(2,1)S(1)} %broadcast_add_fusion.3), channel_id=1, source_target_pairs={{0,224},{16,48},{32,0},{48,80},{64,32},{80,112},{96,64},{112,144},... | collective-permute-start | bytes 688136 | tf_op jit(solution)/shard_map/ppermute | solution.py:323
  64.3 9.3 %collective-permute-start.13 = (bf16[128,896]{1,0:T(8,128)(2,1)S(1)}, bf16[128,896]{1,0:T(8,128)(2,1)S(1)}, u32[]{:S(2)}, u32[]{:S(2)}) collective-permute-start(bf16[128,896]{1,0:T(8,128)(2,1)S(1)} %broadcast_add_fusion.1), channel_id=1, source_target_pairs={{0,32},{16,240},{32,64},{48,16},{64,96},{80,48},{96,128},{112,80},... | collective-permute-start | bytes 688136 | tf_op jit(solution)/shard_map/ppermute | solution.py:322
  67.1 10.4 %collective-permute-start.11 = (bf16[128,896]{1,0:T(8,128)(2,1)S(1)}, bf16[128,896]{1,0:T(8,128)(2,1)S(1)}, u32[]{:S(2)}, u32[]{:S(2)}) collective-permute-start(bf16[128,896]{1,0:T(8,128)(2,1)S(1)} %broadcast_add_fusion.2), channel_id=1, source_target_pairs={{0,224},{16,48},{32,0},{48,80},{64,32},{80,112},{96,64},{112,144},... | collective-permute-start | bytes 688136 | tf_op jit(solution)/shard_map/ppermute | solution.py:323
  73.6 11.2 %collective-permute-start.15 = (bf16[128,896]{1,0:T(8,128)(2,1)S(1)}, bf16[128,896]{1,0:T(8,128)(2,1)S(1)}, u32[]{:S(2)}, u32[]{:S(2)}) collective-permute-start(bf16[128,896]{1,0:T(8,128)(2,1)S(1)} %broadcast_add_fusion), channel_id=1, source_target_pairs={{0,32},{16,240},{32,64},{48,16},{64,96},{80,48},{96,128},{112,80},... | collective-permute-start | bytes 688136 | tf_op jit(solution)/shard_map/ppermute | solution.py:322
  73.7 14.7 %collective-permute-start.14 = (bf16[128,896]{1,0:T(8,128)(2,1)S(1)}, bf16[128,896]{1,0:T(8,128)(2,1)S(1)}, u32[]{:S(2)}, u32[]{:S(2)}) collective-permute-start(bf16[128,896]{1,0:T(8,128)(2,1)S(1)} %broadcast_add_fusion), channel_id=1, source_target_pairs={{0,64},{16,208},{32,96},{48,240},{64,128},{80,16},{96,160},{112,48... | collective-permute-start | bytes 688136 | tf_op jit(solution)/shard_map/ppermute | solution.py:324
  77.5 11.0 %collective-permute-start.12 = (bf16[128,896]{1,0:T(8,128)(2,1)S(1)}, bf16[128,896]{1,0:T(8,128)(2,1)S(1)}, u32[]{:S(2)}, u32[]{:S(2)}) collective-permute-start(bf16[128,896]{1,0:T(8,128)(2,1)S(1)} %collective-permute-done.11.refs_0_), channel_id=1, source_target_pairs={{0,224},{16,48},{32,0},{48,80},{64,32},{80,112},{96,64},{112,144},... | collective-permute-start | bytes 688136 | tf_op jit(solution)/shard_map/ppermute | solution.py:323
  103.1 7.7 %collective-permute-start.16 = (bf16[16,448]{1,0:T(8,128)(2,1)S(1)}, bf16[16,448]{1,0:T(8,128)(2,1)S(1)}, u32[]{:S(2)}, u32[]{:S(2)}) collective-permute-start(bf16[16,448]{1,0:T(8,128)(2,1)S(1)} %combine.1), channel_id=1, source_target_pairs={{7,0},{2,1},{11,32},{6,33},{3,64},{14,65},{12,96},{13,97},{0,128},... | collective-permute-start | bytes 43016 | tf_op jit(solution)/shard_map/ppermute | solution.py:373

commit v4 on v3

--- a/solution.py
+++ b/solution.py
@@ -280,6 +280,22 @@
     )(*blocks, *[stay(t) for t in tables], *ready, *old)
 
 
+def add_kernel(x_ref, y_ref, out_ref):
+    out_ref[...] = x_ref[...] + y_ref[...]
+
+
+def add(x, y):
+    return pl.pallas_call(
+        add_kernel,
+        out_shape=jax.ShapeDtypeStruct(x.shape, x.dtype),
+        in_specs=[VMEM] * 2,
+        out_specs=VMEM,
+        cost_estimate=cost(10 << 30, 1 << 20),
+        compiler_params=limit,
+        name="add",
+    )(x, y)
+
+
 def combine_kernel(got_ref, out_ref):
     parts, rows, wide = got_ref.shape
     feats = out_ref.shape[1]
@@ -343,21 +359,18 @@
     b = down(enc(m2 + dec(b)))
     a = up(enc(p1 + dec(a)))
     b = down(enc(m1 + dec(b)))
-    full = p0 + dec(a) + dec(b)
+    full = add(p0, dec(b)) + dec(a)
 
     block = softmax_of(full, embed_other)
     tables = [embed_own, embed_other]
     mix = lambda order, blocks, old, **kw: mix_of(order, blocks, tables, [], old, **kw)
-    a1 = up(block)
+    a1, b1 = up(block), down(block)
     *state, za, zb = mix((0,), [block], [])
-    b1 = down(block + zb)
-    a2 = up(a1 + za)
+    a2, b2 = up(a1 + za), down(b1 + zb)
     *state, za, zb = mix((7,), [a1], state)
-    b2 = down(b1 + zb)
-    a2_sent = a2 + za
-    a4, a3 = up2(a2_sent), up(a2_sent)
-    b3 = down(b2)
-    *state, _, _ = mix((1, 6), [b1, a2], state)
+    a3, b3 = up(a2 + za), down(b2 + zb)
+    *state, za, _ = mix((1, 6), [b1, a2], state)
+    a4 = up(a3)
     *state, _, _, ready = mix((2, 5), [b2, a3], state, ahead=(3, 4))
     (blocks,) = mix_of((3, 4), [b3, a4], tables, [ready], state)
 

time: 113 us -> 110 us (0.973)
  waiting for transfers between devices: 43.5 us -> 39.1 us
  starting transfers between devices: 31.9 us -> 33.1 us
    ppermute x6 -> x7, waiting for transfers between devices: 21.3 us -> 11.5 us  [on_device(): lax.ppermute(x, 'dp', [(i, (i + side[i]) % size) for i in range(size)])]
    ppermute x6, waiting for transfers between devices: 5.74 us -> 10.5 us  [on_device(): lax.ppermute(x, 'dp', [(i, (i - side[i]) % size) for i in range(size)])]
    ppermute x6 -> x7, starting transfers between devices: 5.57 us -> 1.06 us  [on_device(): lax.ppermute(x, 'dp', [(i, (i + side[i]) % size) for i in range(size)])]
    ppermute x6, starting transfers between devices: 14 us -> 18 us  [on_device(): lax.ppermute(x, 'dp', [(i, (i - side[i]) % size) for i in range(size)])]
    ppermute x2 -> x1, waiting for transfers between devices: 0.01 us -> 3.06 us  [on_device(): lax.ppermute(x, 'dp', [(i, (i + 2 * side[i]) % size) for i in range(size)])]
    ppermute x1, starting transfers between devices: 2.61 us -> 5.01 us  [on_device(): return lax.ppermute(result, ('dp', 'vocab'), flip)]
    ppermute x1, waiting for transfers between devices: 5.11 us -> 2.71 us  [on_device(): return lax.ppermute(result, ('dp', 'vocab'), flip)]
  transfers between devices with their start and end apart: 18 -> 18, of which waited for: 10 -> 13; matrix products, arithmetic and copies ran while one was open for 1% -> 1% of each run, Pallas kernels for 17% -> 18%
where the time goes in v4:
time: 110 us; the launch traced here: 108 us
  waiting for transfers between devices  39.1 us (36%)
  starting transfers between devices  33.1 us (30%)
  Pallas kernels  21.1 us (19%)
  blocking collectives  13.2 us (12%)
    ppermute x6, starting transfers between devices, on_device(): lax.ppermute(x, 'dp', [(i, (i - side[i]) % size) for i in range(size)])  18 us
    all_to_all x1, blocking collectives, on_device(): result = combine(lax.all_to_all(blocks, 'vocab', 0, 0), feats)  13.2 us
    pallas_call x5, Pallas kernels, mix_of(): pl.pallas_call(lambda *refs: mix_kernel(order, ahead, len(blocks), *refs)...  12.1 us
    ppermute x7, waiting for transfers between devices, on_device(): lax.ppermute(x, 'dp', [(i, (i + side[i]) % size) for i in range(size)])  11.5 us
    all_to_all x1, waiting for transfers between devices, on_device(): lax.all_to_all(deal(hidden, chips), 'dp', 0, 0, axis_index_groups=groups)  11.3 us
    ppermute x6, waiting for transfers between devices, on_device(): lax.ppermute(x, 'dp', [(i, (i - side[i]) % size) for i in range(size)])  10.5 us
    all_to_all x1, starting transfers between devices, on_device(): lax.all_to_all(deal(hidden, chips), 'dp', 0, 0, axis_index_groups=groups)  8.48 us
    pallas_call x2, Pallas kernels, logits_of(): pl.pallas_call(lambda *refs: logits_kernel(order, *refs), out_shape=[jax....  6.91 us
  transfers between devices with their start and end apart: 18, of which 13 were waited for; matrix products, arithmetic and copies ran while one was open for 1% of the time, Pallas kernels for 18%

profile of v4, /device:TPU:16, one launch (start us, length us, event | category | flops | bytes accessed | tf_op | source)
XLA Modules:
  0.0 108.4 jit_solution(12174651805761394920)
XLA Ops:
  0.0 0.5 collective-permute-start.8
  0.5 1.6 %deal.1 = bf16[8,16,896]{2,1,0:T(8,128)(2,1)} custom-call(bf16[16,7168]{1,0:T(8,128)(2,1)} %hidden_ref.1), custom_call_target="tpu_custom_call" | custom-call | bytes 524288 | tf_op jit(solution)/shard_map/deal/pallas_call | solution.py:84
  2.1 8.5 %all-to-all-start = ((bf16[8,16,896]{2,1,0:T(8,128)(2,1)}), bf16[8,16,896]{2,1,0:T(8,128)(2,1)S(1)}, u32[]{:S(2)}, u32[]{:S(2)}) async-start(bf16[8,16,896]{2,1,0:T(8,128)(2,1)} %deal.1), calls=%async_computation | async-start | bytes 458752 | tf_op jit(solution)/shard_map/all_to_all | solution.py:345
  10.6 11.3 %all-to-all-done = bf16[8,16,896]{2,1,0:T(8,128)(2,1)S(1)} async-done(((bf16[8,16,896]{2,1,0:T(8,128)(2,1)}), bf16[8,16,896]{2,1,0:T(8,128)(2,1)S(1)}, u32[]{:S(2)}, u32[]{:S(2)}) %all-to-all-start) | async-done | bytes 229408 | tf_op jit(solution)/shard_map/all_to_all | solution.py:345
  22.0 0.1 broadcast_select_fusion
  22.1 2.9 %logits3.1 = (f32[128,896]{1,0:T(8,128)S(1)}, f32[128,896]{1,0:T(8,128)S(1)}, f32[128,896]{1,0:T(8,128)S(1)}) custom-call(bf16[128,448]{1,0:T(8,128)(2,1)S(1)} %get-tuple-element.48.refs_0_, bf16[128,448]{1,0:T(8,128)(2,1)S(1)} %get-tuple-element.47.refs_1_, bf16[448,6656]{1,0:T(8,128)(2,1)} %refs_2_.3, bf16[448,6656]{1,0:T(8,128)(2,1)} %collective-permute-done.refs_3_), custom_call_target="tpu_custom_call" | custom-call | flops 616562688 | bytes 4816896 | tf_op jit(solution)/shard_map/logits3/pallas_call | solution.py:119
  25.1 0.6 collective-permute-start.4
  25.7 2.7 %collective-permute-start.1 = (f16[128,896]{1,0:T(8,128)(2,1)S(1)}, f16[128,896]{1,0:T(8,128)(2,1)S(1)}, u32[]{:S(2)}, u32[]{:S(2)}) collective-permute-start(f16[128,896]{1,0:T(8,128)(2,1)S(1)} %multiply_convert_fusion.6), channel_id=1, source_target_pairs={{0,224},{16,48},{32,0},{48,80},{64,32},{80,112},{96,64},{112,144},... | collective-permute-start | bytes 688136 | tf_op jit(solution)/shard_map/ppermute | solution.py:339
  28.5 0.1 collective-permute-start.5
  28.6 4.0 %logits5.1 = (f32[128,896]{1,0:T(8,128)S(1)}, f32[128,896]{1,0:T(8,128)S(1)}, f32[128,896]{1,0:T(8,128)S(1)}, f32[128,896]{1,0:T(8,128)S(1)}, f32[128,896]{1,0:T(8,128)S(1)}) custom-call(bf16[128,448]{1,0:T(8,128)(2,1)S(1)} %get-tuple-element.48.refs_0_, bf16[128,448]{1,0:T(8,128)(2,1)S(1)} %get-tuple-element.47.refs_1_, bf16[448,6656]{1,0:T(8,128)(2,1)} %refs_2_.3, ...), custom_call_target="tpu_custom_call" | custom-call | flops 1027604480 | bytes 8028160 | tf_op jit(solution)/shard_map/logits5/pallas_call | solution.py:119
  32.6 3.5 %collective-permute-done.1 = f16[128,896]{1,0:T(8,128)(2,1)S(1)} collective-permute-done((f16[128,896]{1,0:T(8,128)(2,1)S(1)}, f16[128,896]{1,0:T(8,128)(2,1)S(1)}, u32[]{:S(2)}, u32[]{:S(2)}) %collective-permute-start.1) | collective-permute-done | bytes 229408 | tf_op jit(solution)/shard_map/ppermute | solution.py:339
  36.1 0.1 multiply_convert_fusion.5
  36.2 1.7 %collective-permute-start.2 = (f16[128,896]{1,0:T(8,128)(2,1)S(1)}, f16[128,896]{1,0:T(8,128)(2,1)S(1)}, u32[]{:S(2)}, u32[]{:S(2)}) collective-permute-start(f16[128,896]{1,0:T(8,128)(2,1)S(1)} %multiply_convert_fusion.5), channel_id=1, source_target_pairs={{0,224},{16,48},{32,0},{48,80},{64,32},{80,112},{96,64},{112,144},... | collective-permute-start | bytes 688136 | tf_op jit(solution)/shard_map/ppermute | solution.py:339
  38.0 3.1 %collective-permute-done.5 = f16[128,896]{1,0:T(8,128)(2,1)S(1)} collective-permute-done((f16[128,896]{1,0:T(8,128)(2,1)S(1)}, f16[128,896]{1,0:T(8,128)(2,1)S(1)}, u32[]{:S(2)}, u32[]{:S(2)}) %collective-permute-start.5) | collective-permute-done | bytes 229408 | tf_op jit(solution)/shard_map/ppermute | solution.py:340
  41.0 0.1 multiply_convert_fusion.1
  41.1 0.1 collective-permute-start.6
  41.2 2.4 %collective-permute-done.2 = f16[128,896]{1,0:T(8,128)(2,1)S(1)} collective-permute-done((f16[128,896]{1,0:T(8,128)(2,1)S(1)}, f16[128,896]{1,0:T(8,128)(2,1)S(1)}, u32[]{:S(2)}, u32[]{:S(2)}) %collective-permute-start.2) | collective-permute-done | bytes 229408 | tf_op jit(solution)/shard_map/ppermute | solution.py:339
  43.6 0.1 multiply_convert_fusion.4
  43.7 3.2 %collective-permute-start.3 = (f16[128,896]{1,0:T(8,128)(2,1)S(1)}, f16[128,896]{1,0:T(8,128)(2,1)S(1)}, u32[]{:S(2)}, u32[]{:S(2)}) collective-permute-start(f16[128,896]{1,0:T(8,128)(2,1)S(1)} %multiply_convert_fusion.4), channel_id=1, source_target_pairs={{0,224},{16,48},{32,0},{48,80},{64,32},{80,112},{96,64},{112,144},... | collective-permute-start | bytes 688136 | tf_op jit(solution)/shard_map/ppermute | solution.py:339
  46.9 1.6 %collective-permute-done.6 = f16[128,896]{1,0:T(8,128)(2,1)S(1)} collective-permute-done((f16[128,896]{1,0:T(8,128)(2,1)S(1)}, f16[128,896]{1,0:T(8,128)(2,1)S(1)}, u32[]{:S(2)}, u32[]{:S(2)}) %collective-permute-start.6) | collective-permute-done | bytes 229408 | tf_op jit(solution)/shard_map/ppermute | solution.py:338
  48.5 0.1 multiply_convert_fusion
  48.6 0.1 collective-permute-start.7
  48.6 2.5 %collective-permute-done.3 = f16[128,896]{1,0:T(8,128)(2,1)S(1)} collective-permute-done((f16[128,896]{1,0:T(8,128)(2,1)S(1)}, f16[128,896]{1,0:T(8,128)(2,1)S(1)}, u32[]{:S(2)}, u32[]{:S(2)}) %collective-permute-start.3) | collective-permute-done | bytes 229408 | tf_op jit(solution)/shard_map/ppermute | solution.py:339
  51.2 0.1 add.100
  51.3 4.6 %collective-permute-done.7 = f16[128,896]{1,0:T(8,128)(2,1)S(1)} collective-permute-done((f16[128,896]{1,0:T(8,128)(2,1)S(1)}, f16[128,896]{1,0:T(8,128)(2,1)S(1)}, u32[]{:S(2)}, u32[]{:S(2)}) %collective-permute-start.7) | collective-permute-done | bytes 229408 | tf_op jit(solution)/shard_map/ppermute | solution.py:338
  55.9 0.1 multiply_add_fusion.full_ref
  55.9 0.3 softmax.1.refs_0_
  56.2 0.1 collective-permute-start.11
  56.3 3.2 %collective-permute-start.9 = (bf16[128,896]{1,0:T(8,128)(2,1)S(1)}, bf16[128,896]{1,0:T(8,128)(2,1)S(1)}, u32[]{:S(2)}, u32[]{:S(2)}) collective-permute-start(bf16[128,896]{1,0:T(8,128)(2,1)S(1)} %softmax.1.refs_0_), channel_id=1, source_target_pairs={{0,224},{16,48},{32,0},{48,80},{64,32},{80,112},{96,64},{112,144},... | collective-permute-start | bytes 688136 | tf_op jit(solution)/shard_map/ppermute | solution.py:339
  59.5 2.1 %mix1.2 = (f32[2,128,512]{2,1,0:T(8,128)S(1)}, f32[128,128]{1,0:T(8,128)S(1)}, bf16[1,896]{1,0:T(2,128)(2,1)S(1)}, bf16[1,896]{1,0:T(2,128)(2,1)S(1)}) custom-call(bf16[128,896]{1,0:T(8,128)(2,1)S(1)} %softmax.1.refs_0_, bf16[448,6656]{1,0:T(8,128)(2,1)} %bitcast.3, bf16[448,6656]{1,0:T(8,128)(2,1)} %collective-permute-done.8.unused_ref.refs_2_.refs_3_), custom_call_target="tpu_custom_call" | custom-call | flops 205520896 | bytes 1605632 | tf_op jit(solution)/shard_map/mix1/pallas_call | solution.py:271
  61.6 1.9 %collective-permute-done.11.refs_0_ = bf16[128,896]{1,0:T(8,128)(2,1)S(1)} collective-permute-done((bf16[128,896]{1,0:T(8,128)(2,1)S(1)}, bf16[128,896]{1,0:T(8,128)(2,1)S(1)}, u32[]{:S(2)}, u32[]{:S(2)}) %collective-permute-start.11) | collective-permute-done | bytes 229408 | tf_op jit(solution)/shard_map/ppermute | solution.py:338
  63.5 0.1 collective-permute-start.13
  63.6 2.1 %mix1.3 = (f32[2,128,512]{2,1,0:T(8,128)S(1)}, f32[128,128]{1,0:T(8,128)S(1)}, bf16[1,896]{1,0:T(2,128)(2,1)S(1)}, bf16[1,896]{1,0:T(2,128)(2,1)S(1)}) custom-call(bf16[128,896]{1,0:T(8,128)(2,1)S(1)} %collective-permute-done.11.refs_0_, bf16[448,6656]{1,0:T(8,128)(2,1)} %bitcast.4, bf16[448,6656]{1,0:T(8,128)(2,1)} %collective-permute-done.8.unused_ref.refs_2_.refs_3_, ...), custom_call_target="tpu_custom_call" | custom-call | flops 205520896 | bytes 1605632 | tf_op jit(solution)/shard_map/mix1/pallas_call | solution.py:271
  65.8 3.3 %collective-permute-start.10 = (bf16[128,896]{1,0:T(8,128)(2,1)S(1)}, bf16[128,896]{1,0:T(8,128)(2,1)S(1)}, u32[]{:S(2)}, u32[]{:S(2)}) collective-permute-start(bf16[128,896]{1,0:T(8,128)(2,1)S(1)} %broadcast_add_fusion.3), channel_id=1, source_target_pairs={{0,224},{16,48},{32,0},{48,80},{64,32},{80,112},{96,64},{112,144},... | collective-permute-start | bytes 688136 | tf_op jit(solution)/shard_map/ppermute | solution.py:339
  69.1 1.7 %collective-permute-done.13.refs_1_ = bf16[128,896]{1,0:T(8,128)(2,1)S(1)} collective-permute-done((bf16[128,896]{1,0:T(8,128)(2,1)S(1)}, bf16[128,896]{1,0:T(8,128)(2,1)S(1)}, u32[]{:S(2)}, u32[]{:S(2)}) %collective-permute-start.13) | collective-permute-done | bytes 229408 | tf_op jit(solution)/shard_map/ppermute | solution.py:338
  70.9 0.1 collective-permute-start.14
  71.0 2.1 %collective-permute-done.10.refs_0_ = bf16[128,896]{1,0:T(8,128)(2,1)S(1)} collective-permute-done((bf16[128,896]{1,0:T(8,128)(2,1)S(1)}, bf16[128,896]{1,0:T(8,128)(2,1)S(1)}, u32[]{:S(2)}, u32[]{:S(2)}) %collective-permute-start.10) | collective-permute-done | bytes 229408 | tf_op jit(solution)/shard_map/ppermute | solution.py:339
  73.1 3.8 %collective-permute-start.12 = (bf16[128,896]{1,0:T(8,128)(2,1)S(1)}, bf16[128,896]{1,0:T(8,128)(2,1)S(1)}, u32[]{:S(2)}, u32[]{:S(2)}) collective-permute-start(bf16[128,896]{1,0:T(8,128)(2,1)S(1)} %broadcast_add_fusion.2), channel_id=1, source_target_pairs={{0,224},{16,48},{32,0},{48,80},{64,32},{80,112},{96,64},{112,144},... | collective-permute-start | bytes 688136 | tf_op jit(solution)/shard_map/ppermute | solution.py:339
  76.8 1.3 %collective-permute-done.14.refs_1_ = bf16[128,896]{1,0:T(8,128)(2,1)S(1)} collective-permute-done((bf16[128,896]{1,0:T(8,128)(2,1)S(1)}, bf16[128,896]{1,0:T(8,128)(2,1)S(1)}, u32[]{:S(2)}, u32[]{:S(2)}) %collective-permute-start.14) | collective-permute-done | bytes 229408 | tf_op jit(solution)/shard_map/ppermute | solution.py:338
  78.2 3.2 %mix2.2 = (f32[2,128,512]{2,1,0:T(8,128)S(1)}, f32[128,128]{1,0:T(8,128)S(1)}, bf16[1,896]{1,0:T(2,128)(2,1)}, bf16[1,896]{1,0:T(2,128)(2,1)}) custom-call(bf16[128,896]{1,0:T(8,128)(2,1)S(1)} %collective-permute-done.9.refs_0_, bf16[128,896]{1,0:T(8,128)(2,1)S(1)} %collective-permute-done.13.refs_1_, bf16[448,6656]{1,0:T(8,128)(2,1)} %bitcast.5, ...), custom_call_target="tpu_custom_call" | custom-call | flops 411041792 | bytes 3211264 | tf_op jit(solution)/shard_map/mix2/pallas_call | solution.py:271
  81.4 3.6 %mix2.3 = (f32[2,128,512]{2,1,0:T(8,128)S(1)}, f32[128,128]{1,0:T(8,128)S(1)}, bf16[1,896]{1,0:T(2,128)(2,1)}, bf16[1,896]{1,0:T(2,128)(2,1)}, bf16[2,2,448,896]{3,2,1,0:T(8,128)(2,1)S(1)}) custom-call(bf16[128,896]{1,0:T(8,128)(2,1)S(1)} %collective-permute-done.10.refs_0_, bf16[128,896]{1,0:T(8,128)(2,1)S(1)} %collective-permute-done.14.refs_1_, ...), custom_call_target="tpu_custom_call" | custom-call | flops 411041792 | bytes 3211264 | tf_op jit(solution)/shard_map/mix2/pallas_call | solution.py:271
  85.0 0.4 collective-permute-done.15.refs_1_
  85.4 1.2 %mix2l.1 = bf16[16,16,512]{2,1,0:T(8,128)(2,1)S(1)} custom-call(bf16[128,896]{1,0:T(8,128)(2,1)S(1)} %collective-permute-done.12.refs_0_, bf16[128,896]{1,0:T(8,128)(2,1)S(1)} %collective-permute-done.15.refs_1_, bf16[2,2,448,896]{3,2,1,0:T(8,128)(2,1)S(1)} %get-tuple-element.44.refs_2_, f32[2,128,512]{2,1,0:T(8,128)S(1)} %get-tuple-element.45.refs_3_, ...), custom_call_target="tpu_custom_call" | custom-call | flops 411041792 | bytes 3211264 | tf_op jit(solution)/shard_map/mix2l/pallas_call | solution.py:271
  86.6 13.2 %all_to_all.10.got_ref = bf16[16,16,512]{2,1,0:T(8,128)(2,1)S(1)} all-to-all(bf16[16,16,512]{2,1,0:T(8,128)(2,1)S(1)} %mix2l.1), channel_id=1, replica_groups=mesh['dp'=16,'vocab'=16] {'vocab'}, dimensions={0} | all-to-all | bytes 524288 | tf_op jit(solution)/shard_map/all_to_all | solution.py:377
  99.9 0.2 combine.1
  100.1 5.0 %collective-permute-start.16 = (bf16[16,448]{1,0:T(8,128)(2,1)S(1)}, bf16[16,448]{1,0:T(8,128)(2,1)S(1)}, u32[]{:S(2)}, u32[]{:S(2)}) collective-permute-start(bf16[16,448]{1,0:T(8,128)(2,1)S(1)} %combine.1), channel_id=1, source_target_pairs={{7,0},{2,1},{11,32},{6,33},{3,64},{14,65},{12,96},{13,97},{0,128},... | collective-permute-start | bytes 43016 | tf_op jit(solution)/shard_map/ppermute | solution.py:386
  105.1 2.7 %collective-permute-done.16 = bf16[16,448]{1,0:T(8,128)(2,1)S(1)} collective-permute-done((bf16[16,448]{1,0:T(8,128)(2,1)S(1)}, bf16[16,448]{1,0:T(8,128)(2,1)S(1)}, u32[]{:S(2)}, u32[]{:S(2)}) %collective-permute-start.16) | collective-permute-done | bytes 14368 | tf_op jit(solution)/shard_map/ppermute | solution.py:386
  107.8 0.6 copy.5
  (19 shorter events, 0.4 us)
Async XLA Ops:
  0.0 22.1 %collective-permute-start = (bf16[448,6656]{1,0:T(8,128)(2,1)}, bf16[448,6656]{1,0:T(8,128)(2,1)}, u32[]{:S(2)}, u32[]{:S(2)}) collective-permute-start(bf16[448,6656]{1,0:T(8,128)(2,1)} %refs_2_.3), channel_id=1, source_target_pairs={{0,16},{16,0},{32,48},{48,32},{64,80},{80,64},{96,112},{112,96},{1... | collective-permute-start | bytes 17891336 | tf_op jit(solution)/shard_map/ppermute | solution.py:336
  0.0 55.9 %collective-permute-start.8 = (bf16[448,6656]{1,0:T(8,128)(2,1)}, bf16[448,6656]{1,0:T(8,128)(2,1)}, u32[]{:S(2)}, u32[]{:S(2)}) collective-permute-start(bf16[448,6656]{1,0:T(8,128)(2,1)} %bitcast.2), channel_id=1, source_target_pairs={{0,16},{16,0},{32,48},{48,32},{64,80},{80,64},{96,112},{112,96},{1... | collective-permute-start | bytes 17891336 | tf_op jit(solution)/shard_map/ppermute | solution.py:336
  2.1 19.8 %all-to-all-start = ((bf16[8,16,896]{2,1,0:T(8,128)(2,1)}), bf16[8,16,896]{2,1,0:T(8,128)(2,1)S(1)}, u32[]{:S(2)}, u32[]{:S(2)}) async-start(bf16[8,16,896]{2,1,0:T(8,128)(2,1)} %deal.1), calls=%async_computation | async-start | bytes 458752 | tf_op jit(solution)/shard_map/all_to_all | solution.py:345
  25.1 12.9 %collective-permute-start.4 = (f16[128,896]{1,0:T(8,128)(2,1)S(1)}, f16[128,896]{1,0:T(8,128)(2,1)S(1)}, u32[]{:S(2)}, u32[]{:S(2)}) collective-permute-start(f16[128,896]{1,0:T(8,128)(2,1)S(1)} %multiply_convert_fusion.3), channel_id=1, source_target_pairs={{0,32},{16,240},{32,64},{48,16},{64,96},{80,48},{96,128},{112,80},... | collective-permute-start | bytes 688136 | tf_op jit(solution)/shard_map/ppermute | solution.py:338
  25.7 10.4 %collective-permute-start.1 = (f16[128,896]{1,0:T(8,128)(2,1)S(1)}, f16[128,896]{1,0:T(8,128)(2,1)S(1)}, u32[]{:S(2)}, u32[]{:S(2)}) collective-permute-start(f16[128,896]{1,0:T(8,128)(2,1)S(1)} %multiply_convert_fusion.6), channel_id=1, source_target_pairs={{0,224},{16,48},{32,0},{48,80},{64,32},{80,112},{96,64},{112,144},... | collective-permute-start | bytes 688136 | tf_op jit(solution)/shard_map/ppermute | solution.py:339
  28.5 12.5 %collective-permute-start.5 = (f16[128,896]{1,0:T(8,128)(2,1)S(1)}, f16[128,896]{1,0:T(8,128)(2,1)S(1)}, u32[]{:S(2)}, u32[]{:S(2)}) collective-permute-start(f16[128,896]{1,0:T(8,128)(2,1)S(1)} %multiply_convert_fusion.2), channel_id=1, source_target_pairs={{0,64},{16,208},{32,96},{48,240},{64,128},{80,16},{96,160},{112,48... | collective-permute-start | bytes 688136 | tf_op jit(solution)/shard_map/ppermute | solution.py:340
  36.2 7.4 %collective-permute-start.2 = (f16[128,896]{1,0:T(8,128)(2,1)S(1)}, f16[128,896]{1,0:T(8,128)(2,1)S(1)}, u32[]{:S(2)}, u32[]{:S(2)}) collective-permute-start(f16[128,896]{1,0:T(8,128)(2,1)S(1)} %multiply_convert_fusion.5), channel_id=1, source_target_pairs={{0,224},{16,48},{32,0},{48,80},{64,32},{80,112},{96,64},{112,144},... | collective-permute-start | bytes 688136 | tf_op jit(solution)/shard_map/ppermute | solution.py:339
  41.1 7.3 %collective-permute-start.6 = (f16[128,896]{1,0:T(8,128)(2,1)S(1)}, f16[128,896]{1,0:T(8,128)(2,1)S(1)}, u32[]{:S(2)}, u32[]{:S(2)}) collective-permute-start(f16[128,896]{1,0:T(8,128)(2,1)S(1)} %multiply_convert_fusion.1), channel_id=1, source_target_pairs={{0,32},{16,240},{32,64},{48,16},{64,96},{80,48},{96,128},{112,80},... | collective-permute-start | bytes 688136 | tf_op jit(solution)/shard_map/ppermute | solution.py:338
  43.7 7.4 %collective-permute-start.3 = (f16[128,896]{1,0:T(8,128)(2,1)S(1)}, f16[128,896]{1,0:T(8,128)(2,1)S(1)}, u32[]{:S(2)}, u32[]{:S(2)}) collective-permute-start(f16[128,896]{1,0:T(8,128)(2,1)S(1)} %multiply_convert_fusion.4), channel_id=1, source_target_pairs={{0,224},{16,48},{32,0},{48,80},{64,32},{80,112},{96,64},{112,144},... | collective-permute-start | bytes 688136 | tf_op jit(solution)/shard_map/ppermute | solution.py:339
  48.6 7.3 %collective-permute-start.7 = (f16[128,896]{1,0:T(8,128)(2,1)S(1)}, f16[128,896]{1,0:T(8,128)(2,1)S(1)}, u32[]{:S(2)}, u32[]{:S(2)}) collective-permute-start(f16[128,896]{1,0:T(8,128)(2,1)S(1)} %multiply_convert_fusion), channel_id=1, source_target_pairs={{0,32},{16,240},{32,64},{48,16},{64,96},{80,48},{96,128},{112,80},... | collective-permute-start | bytes 688136 | tf_op jit(solution)/shard_map/ppermute | solution.py:338
  56.2 7.3 %collective-permute-start.11 = (bf16[128,896]{1,0:T(8,128)(2,1)S(1)}, bf16[128,896]{1,0:T(8,128)(2,1)S(1)}, u32[]{:S(2)}, u32[]{:S(2)}) collective-permute-start(bf16[128,896]{1,0:T(8,128)(2,1)S(1)} %softmax.1.refs_0_), channel_id=1, source_target_pairs={{0,32},{16,240},{32,64},{48,16},{64,96},{80,48},{96,128},{112,80},... | collective-permute-start | bytes 688136 | tf_op jit(solution)/shard_map/ppermute | solution.py:338
  56.3 9.4 %collective-permute-start.9 = (bf16[128,896]{1,0:T(8,128)(2,1)S(1)}, bf16[128,896]{1,0:T(8,128)(2,1)S(1)}, u32[]{:S(2)}, u32[]{:S(2)}) collective-permute-start(bf16[128,896]{1,0:T(8,128)(2,1)S(1)} %softmax.1.refs_0_), channel_id=1, source_target_pairs={{0,224},{16,48},{32,0},{48,80},{64,32},{80,112},{96,64},{112,144},... | collective-permute-start | bytes 688136 | tf_op jit(solution)/shard_map/ppermute | solution.py:339
  63.5 7.3 %collective-permute-start.13 = (bf16[128,896]{1,0:T(8,128)(2,1)S(1)}, bf16[128,896]{1,0:T(8,128)(2,1)S(1)}, u32[]{:S(2)}, u32[]{:S(2)}) collective-permute-start(bf16[128,896]{1,0:T(8,128)(2,1)S(1)} %broadcast_add_fusion.1), channel_id=1, source_target_pairs={{0,32},{16,240},{32,64},{48,16},{64,96},{80,48},{96,128},{112,80},... | collective-permute-start | bytes 688136 | tf_op jit(solution)/shard_map/ppermute | solution.py:338
  65.8 7.3 %collective-permute-start.10 = (bf16[128,896]{1,0:T(8,128)(2,1)S(1)}, bf16[128,896]{1,0:T(8,128)(2,1)S(1)}, u32[]{:S(2)}, u32[]{:S(2)}) collective-permute-start(bf16[128,896]{1,0:T(8,128)(2,1)S(1)} %broadcast_add_fusion.3), channel_id=1, source_target_pairs={{0,224},{16,48},{32,0},{48,80},{64,32},{80,112},{96,64},{112,144},... | collective-permute-start | bytes 688136 | tf_op jit(solution)/shard_map/ppermute | solution.py:339
  70.9 7.3 %collective-permute-start.14 = (bf16[128,896]{1,0:T(8,128)(2,1)S(1)}, bf16[128,896]{1,0:T(8,128)(2,1)S(1)}, u32[]{:S(2)}, u32[]{:S(2)}) collective-permute-start(bf16[128,896]{1,0:T(8,128)(2,1)S(1)} %broadcast_add_fusion), channel_id=1, source_target_pairs={{0,32},{16,240},{32,64},{48,16},{64,96},{80,48},{96,128},{112,80},... | collective-permute-start | bytes 688136 | tf_op jit(solution)/shard_map/ppermute | solution.py:338
  73.1 11.9 %collective-permute-start.12 = (bf16[128,896]{1,0:T(8,128)(2,1)S(1)}, bf16[128,896]{1,0:T(8,128)(2,1)S(1)}, u32[]{:S(2)}, u32[]{:S(2)}) collective-permute-start(bf16[128,896]{1,0:T(8,128)(2,1)S(1)} %broadcast_add_fusion.2), channel_id=1, source_target_pairs={{0,224},{16,48},{32,0},{48,80},{64,32},{80,112},{96,64},{112,144},... | collective-permute-start | bytes 688136 | tf_op jit(solution)/shard_map/ppermute | solution.py:339
  78.2 7.2 %collective-permute-start.15 = (bf16[128,896]{1,0:T(8,128)(2,1)S(1)}, bf16[128,896]{1,0:T(8,128)(2,1)S(1)}, u32[]{:S(2)}, u32[]{:S(2)}) collective-permute-start(bf16[128,896]{1,0:T(8,128)(2,1)S(1)} %collective-permute-done.14.refs_1_), channel_id=1, source_target_pairs={{0,32},{16,240},{32,64},{48,16},{64,96},{80,48},{96,128},{112,80},... | collective-permute-start | bytes 688136 | tf_op jit(solution)/shard_map/ppermute | solution.py:338
  100.1 7.7 %collective-permute-start.16 = (bf16[16,448]{1,0:T(8,128)(2,1)S(1)}, bf16[16,448]{1,0:T(8,128)(2,1)S(1)}, u32[]{:S(2)}, u32[]{:S(2)}) collective-permute-start(bf16[16,448]{1,0:T(8,128)(2,1)S(1)} %combine.1), channel_id=1, source_target_pairs={{7,0},{2,1},{11,32},{6,33},{3,64},{14,65},{12,96},{13,97},{0,128},... | collective-permute-start | bytes 43016 | tf_op jit(solution)/shard_map/ppermute | solution.py:386
